TPU v7x, 32 devices: a whole 2x2x4 slice. The times are simulated.
32 devices in a mesh: lat: 4 (over y, x), ord: 8 (over z, core).
Axes of the slice: x: 2, y: 2, z: 4, core: 2. Of those that a mesh axis runs over, the one named last changes fastest.
Arguments:
- field: bfloat16 [32, 64, 256], P(('lat', 'ord')), may hold values from -6 to 6
- tap_mask: int32 [32, 8, 15], P(('lat', 'ord')), may hold values 0 or 1
- tap_weight: float32 [32, 8, 15], P(('lat', 'ord')), may hold values from -1.4 to 1.4
- basis_mix: bfloat16 [8, 256, 256], replicated, may hold values from -0.125 to 0.125
- order_slots: int32 [32], replicated, may hold values from 0 to 31, each once
- degree_gain: float32 [32, 256], replicated, may hold values from 0.3 to 3
- spectral_mix: bfloat16 [2, 256, 256], replicated, may hold values from -0.25 to 0.25
Outputs:
- spectrum: bfloat16 [32, 32, 2, 256], P('lat', 'ord')
Inputs may be any that keep to these rules, and one draw needn't show every extreme that they name: `order_slots`: each order 0 to 31 stands in exactly one slot.
All inputs are finite; a program needn't handle non-finite values. No bound on the sum of `tap_mask` on one device may be relied on, other than what follows from the above.
Results may differ from a plain program's by a relative error of at most 0.0095.
Values may be sent and summed in bfloat16 or wider, within the bound.
A program may use at most 64 MiB of HBM per device.

v0:
```python
import functools
import math

import jax
import jax.numpy as jnp
from jax import lax
from jax.experimental import pallas as pl
from jax.experimental.pallas import tpu as pltpu
from jax.sharding import PartitionSpec as P

MESH = pl.DeviceIdType.MESH
F32 = jnp.float32
BF16 = jnp.bfloat16
PAD = 8
SLAB = 8


def log2(n):
    assert n & (n - 1) == 0
    return n.bit_length() - 1


def cosine(phase_int, period):
    q = phase_int & (period - 1)
    r = jnp.minimum(q, period - q)
    x = (period // 4 - r).astype(F32) * (2.0 * math.pi / period)
    x2 = x * x
    total = jnp.full_like(x, -1.0 / math.factorial(11))
    for power, sign in ((9, 1.0), (7, -1.0), (5, 1.0), (3, -1.0), (1, 1.0)):
        total = total * x2 + sign / math.factorial(power)
    return total * x


def iota(shape, dim):
    return lax.broadcasted_iota(jnp.int32, shape, dim)


def repeat(count, body):
    if count == 1:
        body(0)
    else:
        pl.loop(0, count)(body)


def kernel(
    dims,
    mask_hbm, weight_hbm, slots_hbm, field_hbm, basis_hbm, gain_hbm, spectral_hbm,
    out_ref,
    mask_ref, weight_ref, slots_ref, rows_in, padded, partial, taps, basis, gain, spectral, grid, table, sent, held, lat_mat,
    local_sem, halo_send, halo_recv, all_send, all_recv, band_sem,
):
    n_lat_dev, n_ord_dev, n_lat, n_lon, n_orders, channels, basis_count = dims
    lat_id = lax.axis_index("lat")
    ord_id = lax.axis_index("ord")
    row_id = lat_id * n_ord_dev + ord_id
    slots_here = n_orders // n_ord_dev
    waves = n_lat // n_lat_dev
    per_slab = min(SLAB // 2, slots_here)
    width = 2 * per_slab
    groups = slots_here // per_slab
    has_prev = row_id > 0
    has_next = row_id < n_lat - 1
    ord_mask = n_ord_dev - 1
    at_first = (ord_id == 0).astype(jnp.int32)
    at_last = (ord_id == ord_mask).astype(jnp.int32)
    prev_dev = (lat_id - at_first, (ord_id + ord_mask) & ord_mask)
    next_dev = (lat_id + at_last, (ord_id + 1) & ord_mask)
    count = n_lat_dev * n_ord_dev
    ord_bits = log2(n_ord_dev)
    assert log2(count) == log2(n_lat_dev) + ord_bits
    far_prev = jnp.logical_and(ord_id == 0, has_prev)
    far_next = jnp.logical_and(ord_id == n_ord_dev - 1, has_next)

    barrier = pltpu.get_barrier_semaphore()

    @pl.when(far_prev)
    def _():
        pl.semaphore_signal(barrier, inc=1, device_id=prev_dev, device_id_type=MESH)

    @pl.when(far_next)
    def _():
        pl.semaphore_signal(barrier, inc=1, device_id=next_dev, device_id_type=MESH)

    for step in range(n_ord_dev - 1, 0, -1):
        pl.semaphore_signal(barrier, inc=1, device_id=(lat_id, ord_id ^ step), device_id_type=MESH)
    for step in range(1, n_lat_dev):
        pl.semaphore_signal(barrier, inc=1, device_id=(lat_id ^ step, ord_id), device_id_type=MESH)

    own_copy = pltpu.make_async_copy(field_hbm, rows_in.at[pl.ds(1, 1)], local_sem.at[0])
    basis_copy = pltpu.make_async_copy(basis_hbm, basis, local_sem.at[1])
    gain_copy = pltpu.make_async_copy(
        gain_hbm.at[pl.ds(pl.multiple_of(lat_id * waves, waves), waves)], gain, local_sem.at[2]
    )
    spectral_copy = pltpu.make_async_copy(spectral_hbm, spectral, local_sem.at[3])
    mask_copy = pltpu.make_async_copy(mask_hbm, mask_ref, local_sem.at[4])
    weight_copy = pltpu.make_async_copy(weight_hbm, weight_ref, local_sem.at[5])
    slots_copy = pltpu.make_async_copy(slots_hbm, slots_ref, local_sem.at[6])
    slots_copy.start()
    mask_copy.start()
    weight_copy.start()
    own_copy.start()
    basis_copy.start()
    gain_copy.start()
    spectral_copy.start()

    @pl.when(jnp.logical_not(has_prev))
    def _():
        rows_in[0] = jnp.zeros(rows_in.shape[1:], BF16)

    @pl.when(jnp.logical_not(has_next))
    def _():
        rows_in[2] = jnp.zeros(rows_in.shape[1:], BF16)

    slots_copy.wait()
    orders = slots_ref[...]

    def pick(slot_of_row):
        found = iota((slot_of_row.shape[0], n_orders), 1) == slot_of_row
        return jnp.sum(jnp.where(found, orders.astype(F32), 0.0), axis=1, keepdims=True).astype(jnp.int32)

    block_rows = table.shape[0]

    def dft_block(start):
        row = iota((block_rows, 1), 0) + start
        order = pick(row >> 1)
        phase = order * iota((block_rows, n_lon), 1) + (n_lon // 4) * (row & 1)
        table[...] = (cosine(phase, n_lon) * (1.0 / math.sqrt(n_lon))).astype(BF16)

    lat_rows = min(n_lat, 256 // width)
    out_rows = waves * width

    def lat_block(group, part):
        row = iota((out_rows, 1), 0)
        col = iota((1, lat_rows * width), 1)
        wave = (row >> log2(width)) + lat_id * waves
        slot = (row & (width - 1)) >> 1
        order = pick(slot + ord_id * slots_here + group * per_slab)
        lat = (col >> log2(width)) + part * lat_rows
        phase = wave * (2 * lat + 1) + jnp.where((order & 1) == 0, 0, 3 * n_lat)
        value = cosine(phase, 4 * n_lat) * math.sqrt(2.0 / n_lat)
        apart = (row & (width - 1)) ^ (col & (width - 1))
        straight = jnp.where(apart == 0, value, 0.0)
        turned = jnp.where(apart == 1, jnp.where((row & 1) == 0, -value, value), 0.0)
        lat_mat[:out_rows] = straight.astype(BF16)
        lat_mat[out_rows:] = turned.astype(BF16)

    single_dft = block_rows == 2 * n_orders
    single_lat = groups == 1 and lat_rows == n_lat
    if single_dft:
        dft_block(0)

    own_copy.wait()
    pl.semaphore_wait(
        barrier, (n_ord_dev - 1) + (n_lat_dev - 1) + far_prev.astype(jnp.int32) + far_next.astype(jnp.int32)
    )

    to_next = pltpu.make_async_remote_copy(
        src_ref=rows_in.at[pl.ds(1, 1)], dst_ref=rows_in.at[pl.ds(0, 1)], send_sem=halo_send.at[0],
        recv_sem=halo_recv.at[0], device_id=next_dev, device_id_type=MESH,
    )
    to_prev = pltpu.make_async_remote_copy(
        src_ref=rows_in.at[pl.ds(1, 1)], dst_ref=rows_in.at[pl.ds(2, 1)], send_sem=halo_send.at[1],
        recv_sem=halo_recv.at[1], device_id=prev_dev, device_id_type=MESH,
    )
    pl.when(has_next)(to_next.start)
    pl.when(has_prev)(to_prev.start)
    for step in range(1, n_lat_dev):
        pl.semaphore_signal(band_sem, inc=1, device_id=(lat_id ^ step, ord_id), device_id_type=MESH)
    if single_lat:
        lat_block(0, 0)

    def spread(which):
        row = rows_in[which].astype(F32)
        padded[which, pl.ds(PAD, n_lon)] = row
        padded[which, pl.ds(0, PAD)] = row[n_lon - PAD:]
        padded[which, pl.ds(PAD + n_lon, PAD)] = row[:PAD]

    lon_block = min(n_lon, 64)
    lon_piece = 16

    def tap_terms(lat_steps, block, piece, b, total):
        first = block * lon_block + piece * lon_piece
        for lat_step in lat_steps:
            if isinstance(block, int):
                window = padded[lat_step, first: first + lon_piece + 2 * PAD]
            else:
                window = padded[lat_step, pl.ds(pl.multiple_of(first, lon_piece), lon_piece + 2 * PAD)]
            for lon_step in range(5):
                tap = 5 * lat_step + lon_step
                shifted = window[PAD + lon_step - 2: PAD + lon_step - 2 + lon_piece]
                term = (mask_ref[0, b, tap].astype(F32) * weight_ref[0, b, tap]) * shifted
                total = term if total is None else total + term
        return total

    def place(block, piece):
        first = block * lon_block + piece * lon_piece
        return pl.ds(first if isinstance(block, int) else pl.multiple_of(first, lon_piece), lon_piece)

    def middle(block):
        for piece in range(lon_block // lon_piece):
            for b in range(basis_count):
                partial[b, place(block, piece)] = tap_terms((1,), block, piece, b, None)

    def convolve(block):
        for piece in range(lon_block // lon_piece):
            for b in range(basis_count):
                total = tap_terms((0, 2), block, piece, b, partial[b, place(block, piece)])
                taps[pl.ds(piece * lon_piece, lon_piece), pl.ds(b * channels, channels)] = total.astype(BF16)
        mixed = jnp.dot(
            taps[...], basis[...].reshape(basis_count * channels, channels), preferred_element_type=F32
        )
        start = block * lon_block if isinstance(block, int) else pl.multiple_of(block * lon_block, lon_block)
        grid[pl.ds(start, lon_block)] = mixed.astype(BF16)

    spread(1)
    mask_copy.wait()
    weight_copy.wait()
    repeat(n_lon // lon_block, middle)
    basis_copy.wait()
    pl.when(has_prev)(to_next.wait_recv)
    spread(0)
    pl.when(has_next)(to_prev.wait_recv)
    spread(2)
    repeat(n_lon // lon_block, convolve)

    slabs = block_rows // width

    def transform(block):
        if not single_dft:
            dft_block(block * block_rows)
        rows = jnp.dot(table[...], grid[...], preferred_element_type=F32).astype(BF16)
        sent[pl.ds(block * slabs, slabs)] = rows.reshape(slabs, width, channels)

    repeat(2 * n_orders // block_rows, transform)

    def send(step):
        lat_step, ord_step = step >> ord_bits, step & ord_mask
        target = (lat_id ^ lat_step, ord_id ^ ord_step)
        pltpu.make_async_remote_copy(
            src_ref=sent.at[pl.ds(target[1] * groups, groups)], dst_ref=held.at[:, row_id],
            send_sem=all_send.at[0], recv_sem=all_recv.at[0],
            device_id=target, device_id_type=MESH,
        ).start()

    pl.semaphore_wait(band_sem, n_lat_dev - 1)
    if count <= 64:
        for step in sorted(range(1, count), key=lambda step: (-(step & ord_mask), -step)):
            send(step)
    else:
        pl.loop(1, count)(send)
    held[:, row_id] = sent[pl.ds(ord_id * groups, groups)]
    pl.when(has_next)(to_next.wait_send)
    pl.when(has_prev)(to_prev.wait_send)
    gain_copy.wait()
    spectral_copy.wait()
    arrivals = pltpu.make_async_remote_copy(
        src_ref=held.at[:, pl.ds(0, count - 1)], dst_ref=held.at[:, pl.ds(0, count - 1)],
        send_sem=all_send.at[0], recv_sem=all_recv.at[0],
        device_id=(lat_id, ord_id ^ 1), device_id_type=MESH,
    )
    arrivals.wait_recv()

    def latitude(group, part):
        rows = held[group, pl.ds(part * lat_rows, lat_rows)].reshape(lat_rows * width, channels)
        return jnp.dot(lat_mat[...], rows, preferred_element_type=F32)

    def finish(group):
        if single_lat:
            total = latitude(group, 0)
        else:
            def add(part, so_far):
                lat_block(group, part)
                return so_far + latitude(group, part)

            total = lax.fori_loop(
                0, n_lat // lat_rows, add, jnp.zeros((2 * out_rows, channels), F32)
            )
        gains = jnp.broadcast_to(gain[...][:, None, :], (waves, width, channels)).reshape(out_rows, channels)
        straight = (total[:out_rows] * gains).astype(BF16)
        turned = (total[out_rows:] * gains).astype(BF16)
        result = jnp.dot(straight, spectral[0], preferred_element_type=F32) + jnp.dot(
            turned, spectral[1], preferred_element_type=F32
        )
        out_ref[group] = result.astype(BF16)

    repeat(groups, finish)
    arrivals.wait_send()


def per_device(field, tap_mask, tap_weight, basis_mix, order_slots, degree_gain, spectral_mix):
    rows_here, n_lon, channels = field.shape
    assert rows_here == 1
    basis_count = basis_mix.shape[0]
    n_lat = degree_gain.shape[0]
    n_orders = order_slots.shape[0]
    n_lat_dev = lax.axis_size("lat")
    n_ord_dev = lax.axis_size("ord")
    slots_here = n_orders // n_ord_dev
    waves = n_lat // n_lat_dev
    per_slab = min(SLAB // 2, slots_here)
    width = 2 * per_slab
    groups = slots_here // per_slab
    lat_rows = min(n_lat, 256 // width)
    block_rows = min(2 * n_orders, 64)
    lon_block = min(n_lon, 64)
    out_rows = waves * width
    dims = (n_lat_dev, n_ord_dev, n_lat, n_lon, n_orders, channels, basis_count)
    vmem = pl.BlockSpec(memory_space=pltpu.VMEM)
    hbm = pl.BlockSpec(memory_space=pltpu.HBM)
    result = pl.pallas_call(
        functools.partial(kernel, dims),
        out_shape=pltpu.VMEM((groups, out_rows, channels), BF16),
        in_specs=[hbm] * 7,
        out_specs=vmem,
        scratch_shapes=[
            pltpu.SMEM(tap_mask.shape, jnp.int32),
            pltpu.SMEM(tap_weight.shape, F32),
            pltpu.VMEM((1, n_orders), jnp.int32),
            pltpu.VMEM((3, n_lon, channels), BF16),
            pltpu.VMEM((3, n_lon + 2 * PAD, channels), F32),
            pltpu.VMEM((basis_count, n_lon, channels), F32),
            pltpu.VMEM((lon_block, basis_count * channels), BF16),
            pltpu.VMEM((basis_count, channels, channels), BF16),
            pltpu.VMEM((waves, channels), F32),
            pltpu.VMEM((2, channels, channels), BF16),
            pltpu.VMEM((n_lon, channels), BF16),
            pltpu.VMEM((block_rows, n_lon), BF16),
            pltpu.VMEM((n_ord_dev * groups, width, channels), BF16),
            pltpu.VMEM((groups, n_lat, width, channels), BF16),
            pltpu.VMEM((2 * out_rows, lat_rows * width), BF16),
            pltpu.SemaphoreType.DMA((7,)),
            pltpu.SemaphoreType.DMA((2,)),
            pltpu.SemaphoreType.DMA((2,)),
            pltpu.SemaphoreType.DMA((1,)),
            pltpu.SemaphoreType.DMA((1,)),
            pltpu.SemaphoreType.REGULAR,
        ],
        compiler_params=pltpu.CompilerParams(
            collective_id=0, has_side_effects=True, vmem_limit_bytes=63 * 1024 * 1024
        ),
    )(*[pltpu.with_memory_space_constraint(x, pltpu.HBM) for x in (tap_mask, tap_weight, order_slots.reshape(1, n_orders), field, basis_mix, degree_gain, spectral_mix)])
    result = result.reshape(groups, waves, per_slab, 2, channels)
    return jnp.swapaxes(result, 0, 1).reshape(waves, slots_here, 2, channels)


def solution(mesh):
    in_specs = (
        P(("lat", "ord"), None, None),
        P(("lat", "ord"), None, None),
        P(("lat", "ord"), None, None),
        P(),
        P(),
        P(),
        P(),
    )
    out_specs = P("lat", "ord", None, None)
    return jax.shard_map(
        per_device, mesh=mesh, in_specs=in_specs, out_specs=out_specs, check_vma=False
    )
```

profile of v0, /device:TPU:0, one launch (start us, length us, event | category | flops | bytes accessed | tf_op | source)
XLA Modules:
  0.0 15.9 jit_solution(3026934590300383133)
XLA Ops:
  0.0 15.2 %shard_map.73 = bf16[1,64,256]{2,1,0:T(8,128)(2,1)S(1)} custom-call(s32[1,8,15]{2,1,0:T(8,128)} %mask_hbm.1, f32[1,8,15]{2,1,0:T(8,128)} %weight_hbm.1, s32[1,32]{1,0:T(1,128)} %bitcast.1, bf16[1,64,256]{2,1,0:T(8,128)(2,1)} %field_hbm.1, bf16[8,256,256]{2,1,0:T(8,128)(2,1)} %basis_hbm.1, f32[32,256]{1,0:T(8,128)} %gain_hbm.1, bf16[2,256,256]{2,1,0:T(8,128)(2,1)} %spectral_hbm.1), custom_call_target="tpu_custom_call" | custom-call | tf_op jit(solution)/shard_map/pallas_call | solution.py:310
  15.2 0.6 %reshape_transpose_reshape.3 = bf16[8,4,2,256]{3,2,1,0:T(2,128)(2,1)} reshape(bf16[1,64,256]{2,1,0:T(8,128)(2,1)S(1)} %shard_map.73) | data formatting | bytes 65536 | tf_op jit(solution)/shard_map/reshape;transpose;reshape | solution.py:343
where the time goes:
time: 16 us; the launch traced here: 15.9 us
  Pallas kernels  15.2 us (95%)
  local copies, waits for them, and re-layouts  0.63 us (4%)
    pallas_call x1, Pallas kernels, per_device(): pl.pallas_call(functools.partial(kernel, dims), out_shape=pltpu.VMEM((gro...  15.2 us
    another operation x1, local copies, waits for them, and re-layouts, per_device(): return jnp.swapaxes(result, 0, 1).reshape(waves, slots_here, 2, channels)  0.63 us

commit v1 on v0

v1 whole, which is shorter than its diff:
```python
import functools
import math

import jax
import jax.numpy as jnp
from jax import lax
from jax.experimental import pallas as pl
from jax.experimental.pallas import tpu as pltpu
from jax.sharding import PartitionSpec as P

MESH = pl.DeviceIdType.MESH
F32 = jnp.float32
BF16 = jnp.bfloat16
SLAB = 8
COLUMNS = 256
LANES = 128


def log2(n):
    assert n & (n - 1) == 0
    return n.bit_length() - 1


def cosine(phase_int, period):
    q = phase_int & (period - 1)
    r = jnp.minimum(q, period - q)
    x = (period // 4 - r).astype(F32) * (2.0 * math.pi / period)
    x2 = x * x
    total = jnp.full_like(x, -1.0 / math.factorial(11))
    for power, sign in ((9, 1.0), (7, -1.0), (5, 1.0), (3, -1.0), (1, 1.0)):
        total = total * x2 + sign / math.factorial(power)
    return total * x


def iota(shape, dim):
    return lax.broadcasted_iota(jnp.int32, shape, dim)


def repeat(count, body):
    if count == 1:
        body(0)
    else:
        pl.loop(0, count)(body)


def kernel(
    dims,
    mask_hbm, weight_hbm, slots_hbm, field_hbm, basis_hbm, gain_hbm, spectral_hbm,
    out_ref,
    mask_ref, weight_ref, slots_ref, slots_smem, field, basis, gain, spectral, table, filt, sent, held, lat_tab, left, mixed,
    local_sem, filt_send, filt_recv, all_send, all_recv,
):
    n_lat_dev, n_ord_dev, n_lat, n_lon, n_orders, channels, basis_count = dims
    lat_id = lax.axis_index("lat")
    ord_id = lax.axis_index("ord")
    row_id = lat_id * n_ord_dev + ord_id
    slots_here = n_orders // n_ord_dev
    waves = n_lat // n_lat_dev
    per_slab = min(SLAB // 2, slots_here)
    width = 2 * per_slab
    groups = slots_here // per_slab
    count = n_lat_dev * n_ord_dev
    ord_mask = n_ord_dev - 1
    ord_bits = log2(n_ord_dev)
    lat_rows = min(n_lat, COLUMNS // width)
    parts = n_lat // lat_rows
    cols = lat_rows * width
    out_rows = waves * width

    def each_target(body):
        if count <= 64:
            for step in sorted(range(1, count), key=lambda step: (-(step & ord_mask), -step)):
                body((lat_id ^ (step >> ord_bits), ord_id ^ (step & ord_mask)))
        else:
            def one(step):
                body((lat_id ^ (step >> ord_bits), ord_id ^ (step & ord_mask)))

            pl.loop(1, count)(one)

    slots_copy = pltpu.make_async_copy(slots_hbm, slots_ref, local_sem.at[0])
    field_copy = pltpu.make_async_copy(field_hbm, field, local_sem.at[1])
    mask_copy = pltpu.make_async_copy(mask_hbm, mask_ref, local_sem.at[2])
    weight_copy = pltpu.make_async_copy(weight_hbm, weight_ref, local_sem.at[3])
    smem_copy = pltpu.make_async_copy(slots_hbm, slots_smem, local_sem.at[4])
    gain_copy = pltpu.make_async_copy(
        gain_hbm.at[pl.ds(pl.multiple_of(lat_id * waves, waves), waves)], gain, local_sem.at[5]
    )
    spectral_copy = pltpu.make_async_copy(spectral_hbm, spectral, local_sem.at[6])
    basis_copy = pltpu.make_async_copy(basis_hbm, basis, local_sem.at[7])
    slots_copy.start()
    field_copy.start()
    mask_copy.start()
    weight_copy.start()
    smem_copy.start()
    basis_copy.start()
    gain_copy.start()
    spectral_copy.start()

    barrier = pltpu.get_barrier_semaphore()

    def greet(target):
        pl.semaphore_signal(barrier, inc=1, device_id=target, device_id_type=MESH)

    each_target(greet)

    filt[0] = jnp.zeros((1, LANES), F32)
    filt[n_lat + 1] = jnp.zeros((1, LANES), F32)

    slots_copy.wait()
    orders = slots_ref[...]
    block_rows = table.shape[0]

    def dft_block(start):
        row = iota((block_rows, 1), 0) + start
        found = iota((block_rows, n_orders), 1) == row >> 1
        order = jnp.sum(jnp.where(found, orders.astype(F32), 0.0), axis=1, keepdims=True).astype(jnp.int32)
        phase = order * iota((block_rows, n_lon), 1) + (n_lon // 4) * (row & 1)
        table[...] = (cosine(phase, n_lon) * (1.0 / math.sqrt(n_lon))).astype(BF16)

    single_dft = block_rows == 2 * n_orders
    if single_dft:
        dft_block(0)
    slabs = block_rows // width

    mask_copy.wait()
    weight_copy.wait()
    taps = mask_ref[0].astype(F32) * weight_ref[0]
    tap_count = taps.shape[1]
    lane = iota((basis_count, LANES), 1)
    spread = jnp.zeros((basis_count, LANES), F32)
    for tap in range(tap_count):
        spread = jnp.where(lane // basis_count == tap, taps[:, tap:tap + 1], spread)
    spread = jnp.where(lane % basis_count == iota((basis_count, LANES), 0), spread, 0.0)
    filt[row_id + 1] = jnp.sum(spread, axis=0, keepdims=True)

    field_copy.wait()

    def transform(block):
        if not single_dft:
            dft_block(block * block_rows)
        rows = jnp.dot(table[...], field[0], preferred_element_type=F32).astype(BF16)
        sent[pl.ds(block * slabs, slabs)] = rows.reshape(slabs, width, channels)

    repeat(2 * n_orders // block_rows, transform)

    pl.semaphore_wait(barrier, count - 1)

    def send(target):
        pltpu.make_async_remote_copy(
            src_ref=filt.at[row_id + 1], dst_ref=filt.at[row_id + 1],
            send_sem=filt_send.at[0], recv_sem=filt_recv.at[0],
            device_id=target, device_id_type=MESH,
        ).start()
        pltpu.make_async_remote_copy(
            src_ref=sent.at[pl.ds(target[1] * groups, groups)], dst_ref=held.at[:, row_id],
            send_sem=all_send.at[0], recv_sem=all_recv.at[0],
            device_id=target, device_id_type=MESH,
        ).start()

    each_target(send)
    held[:, row_id] = sent[pl.ds(ord_id * groups, groups)]

    smem_copy.wait()

    def lane_orders(group):
        place = (iota((1, cols), 1) & (width - 1)) >> 1
        order = jnp.zeros((1, cols), jnp.int32)
        for slot in range(per_slab):
            order = jnp.where(place == slot, slots_smem[0, ord_id * slots_here + group * per_slab + slot], order)
        return order

    def lat_tables(group, part):
        order = lane_orders(group)
        col = iota((1, cols), 1)
        row = iota((out_rows, 1), 0)
        wave = (row >> log2(width)) + lat_id * waves
        same = ((row & (width - 1)) >> 1) == ((col & (width - 1)) >> 1)
        for step in range(3):
            lat = (col >> log2(width)) + part * lat_rows + 1 - step
            phase = wave * (2 * lat + 1) + jnp.where((order & 1) == 0, 0, 3 * n_lat)
            value = cosine(phase, 4 * n_lat) * math.sqrt(2.0 / n_lat)
            lat_tab[step] = jnp.where(same, value, 0.0)

    def tap_factors(group):
        order = lane_orders(group)
        row = iota((16, cols), 0)
        lon_step = (row & 7) - 2
        part_of = iota((16, cols), 1) & 1
        phase = order * lon_step + (n_lon // 4) * (part_of - (row >> 3))
        return cosine(phase, n_lon)

    single_lat = groups == 1 and parts == 1
    if single_lat:
        lat_tables(0, 0)
        factors = tap_factors(0)

    gain_copy.wait()
    spectral_copy.wait()
    basis_copy.wait()
    filt_arrivals = pltpu.make_async_remote_copy(
        src_ref=filt.at[pl.ds(0, count - 1)], dst_ref=filt.at[pl.ds(0, count - 1)],
        send_sem=filt_send.at[0], recv_sem=filt_recv.at[0],
        device_id=(lat_id, ord_id ^ 1), device_id_type=MESH,
    )
    arrivals = pltpu.make_async_remote_copy(
        src_ref=held.at[:, pl.ds(0, count - 1)], dst_ref=held.at[:, pl.ds(0, count - 1)],
        send_sem=all_send.at[0], recv_sem=all_recv.at[0],
        device_id=(lat_id, ord_id ^ 1), device_id_type=MESH,
    )
    filt_arrivals.wait_recv()

    def build_left(part, factors):
        window = filt[pl.ds(part * lat_rows, lat_rows + 2)].reshape(lat_rows + 2, LANES)
        high = window.astype(BF16)
        low = (window - high.astype(F32)).astype(BF16)
        both = jnp.concatenate([high.astype(F32), low.astype(F32)], axis=0).T.astype(BF16)
        row = iota((lat_rows + 2, cols), 0)
        lat = iota((lat_rows + 2, cols), 1) >> log2(width)
        real, imag = [], []
        for step in range(3):
            chosen = (row == lat + 2 - step).astype(F32)
            chosen = jnp.concatenate([chosen, chosen], axis=0).astype(BF16)
            first = 5 * step * basis_count
            wide = jnp.dot(both[first:first + 5 * basis_count], chosen, preferred_element_type=F32)
            sums = [None, None]
            for lon_step in range(5):
                values = wide[lon_step * basis_count:(lon_step + 1) * basis_count]
                for which in range(2):
                    term = values * factors[8 * which + lon_step:8 * which + lon_step + 1]
                    sums[which] = term if sums[which] is None else sums[which] + term
            real.append(sums[0])
            imag.append(sums[1])
        even = (iota((width, cols), 0) & 1) == 0
        for b in range(basis_count):
            total = None
            for step in range(3):
                turn = jnp.where(even, real[step][b:b + 1], imag[step][b:b + 1])
                term = lat_tab[step].reshape(waves, width, cols) * turn[None]
                total = term if total is None else total + term
            left[pl.ds(b * out_rows, out_rows)] = total.reshape(out_rows, cols).astype(BF16)

    def latitude(group, part):
        rows = held[group, pl.ds(part * lat_rows, lat_rows)].reshape(cols, channels)
        return jnp.dot(left[...], rows, preferred_element_type=F32)

    def finish(group):
        if single_lat:
            total = latitude(group, 0)
        else:
            factors_here = tap_factors(group)
            mixed[...] = jnp.zeros(mixed.shape, F32)

            def add(part):
                lat_tables(group, part)
                build_left(part, factors_here)
                mixed[...] += latitude(group, part)

            pl.loop(0, parts)(add)
            total = mixed[...]
        total = total.astype(BF16)
        flat = jnp.concatenate([total[b * out_rows:(b + 1) * out_rows] for b in range(basis_count)], axis=1)
        coefficients = jnp.dot(flat, basis[...].reshape(basis_count * channels, channels), preferred_element_type=F32)
        scaled = (coefficients.reshape(waves, width, channels) * gain[...][:, None, :]).astype(BF16)
        scaled = scaled.reshape(out_rows, channels)
        straight = jnp.dot(scaled, spectral[0], preferred_element_type=F32)
        turned = jnp.dot(scaled, spectral[1], preferred_element_type=F32).reshape(waves, width, channels)
        even = (iota((1, width, channels), 1) & 1) == 0
        turned = jnp.where(even, -pltpu.roll(turned, width - 1, 1), pltpu.roll(turned, 1, 1))
        out_ref[group] = (straight + turned.reshape(out_rows, channels)).astype(BF16)

    if single_lat:
        build_left(0, factors)
    arrivals.wait_recv()
    repeat(groups, finish)
    filt_arrivals.wait_send()
    arrivals.wait_send()


def per_device(field, tap_mask, tap_weight, basis_mix, order_slots, degree_gain, spectral_mix):
    rows_here, n_lon, channels = field.shape
    assert rows_here == 1
    basis_count = basis_mix.shape[0]
    n_lat = degree_gain.shape[0]
    n_orders = order_slots.shape[0]
    n_lat_dev = lax.axis_size("lat")
    n_ord_dev = lax.axis_size("ord")
    slots_here = n_orders // n_ord_dev
    waves = n_lat // n_lat_dev
    per_slab = min(SLAB // 2, slots_here)
    width = 2 * per_slab
    groups = slots_here // per_slab
    lat_rows = min(n_lat, COLUMNS // width)
    block_rows = min(2 * n_orders, 64)
    out_rows = waves * width
    single = groups == 1 and lat_rows == n_lat
    dims = (n_lat_dev, n_ord_dev, n_lat, n_lon, n_orders, channels, basis_count)
    vmem = pl.BlockSpec(memory_space=pltpu.VMEM)
    hbm = pl.BlockSpec(memory_space=pltpu.HBM)
    result = pl.pallas_call(
        functools.partial(kernel, dims),
        out_shape=pltpu.VMEM((groups, out_rows, channels), BF16),
        in_specs=[hbm] * 7,
        out_specs=vmem,
        scratch_shapes=[
            pltpu.VMEM(tap_mask.shape, jnp.int32),
            pltpu.VMEM(tap_weight.shape, F32),
            pltpu.VMEM((1, n_orders), jnp.int32),
            pltpu.SMEM((1, n_orders), jnp.int32),
            pltpu.VMEM((1, n_lon, channels), BF16),
            pltpu.VMEM((basis_count, channels, channels), BF16),
            pltpu.VMEM((waves, channels), F32),
            pltpu.VMEM((2, channels, channels), BF16),
            pltpu.VMEM((block_rows, n_lon), BF16),
            pltpu.VMEM((n_lat + 2, 1, LANES), F32),
            pltpu.VMEM((n_ord_dev * groups, width, channels), BF16),
            pltpu.VMEM((groups, n_lat, width, channels), BF16),
            pltpu.VMEM((3, out_rows, lat_rows * width), F32),
            pltpu.VMEM((basis_count * out_rows, lat_rows * width), BF16),
            pltpu.VMEM((8, LANES) if single else (basis_count * out_rows, channels), F32),
            pltpu.SemaphoreType.DMA((8,)),
            pltpu.SemaphoreType.DMA((1,)),
            pltpu.SemaphoreType.DMA((1,)),
            pltpu.SemaphoreType.DMA((1,)),
            pltpu.SemaphoreType.DMA((1,)),
        ],
        compiler_params=pltpu.CompilerParams(
            collective_id=0, has_side_effects=True, vmem_limit_bytes=63 * 1024 * 1024
        ),
    )(*[pltpu.with_memory_space_constraint(x, pltpu.HBM) for x in (tap_mask, tap_weight, order_slots.reshape(1, n_orders), field, basis_mix, degree_gain, spectral_mix)])
    result = result.reshape(groups, waves, per_slab, 2, channels)
    return jnp.swapaxes(result, 0, 1).reshape(waves, slots_here, 2, channels)


def solution(mesh):
    in_specs = (
        P(("lat", "ord"), None, None),
        P(("lat", "ord"), None, None),
        P(("lat", "ord"), None, None),
        P(),
        P(),
        P(),
        P(),
    )
    out_specs = P("lat", "ord", None, None)
    return jax.shard_map(
        per_device, mesh=mesh, in_specs=in_specs, out_specs=out_specs, check_vma=False
    )
```

time: 16 us -> 13.6 us (0.85)
  Pallas kernels: 15.2 us -> 12.8 us
    pallas_call x1, Pallas kernels: 15.2 us -> 12.8 us  [per_device(): pl.pallas_call(functools.partial(kernel, dims), out_shape=pltpu.VMEM((gro...]
where the time goes in v1:
time: 13.6 us; the launch traced here: 13.4 us
  Pallas kernels  12.8 us (94%)
  local copies, waits for them, and re-layouts  0.63 us (5%)
    pallas_call x1, Pallas kernels, per_device(): pl.pallas_call(functools.partial(kernel, dims), out_shape=pltpu.VMEM((gro...  12.8 us
    another operation x1, local copies, waits for them, and re-layouts, per_device(): return jnp.swapaxes(result, 0, 1).reshape(waves, slots_here, 2, channels)  0.63 us

profile of v1, /device:TPU:0, one launch (start us, length us, event | category | flops | bytes accessed | tf_op | source)
XLA Modules:
  0.0 13.4 jit_solution(8101145506000172825)
XLA Ops:
  0.0 12.8 %shard_map.73 = bf16[1,64,256]{2,1,0:T(8,128)(2,1)S(1)} custom-call(s32[1,8,15]{2,1,0:T(8,128)} %mask_hbm.1, f32[1,8,15]{2,1,0:T(8,128)} %weight_hbm.1, s32[1,32]{1,0:T(1,128)} %bitcast.1, bf16[1,64,256]{2,1,0:T(8,128)(2,1)} %field_hbm.1, bf16[8,256,256]{2,1,0:T(8,128)(2,1)} %basis_hbm.1, f32[32,256]{1,0:T(8,128)} %gain_hbm.1, bf16[2,256,256]{2,1,0:T(8,128)(2,1)} %spectral_hbm.1), custom_call_target="tpu_custom_call" | custom-call | tf_op jit(solution)/shard_map/pallas_call | solution.py:299
  12.8 0.6 %reshape_transpose_reshape.3 = bf16[8,4,2,256]{3,2,1,0:T(2,128)(2,1)} reshape(bf16[1,64,256]{2,1,0:T(8,128)(2,1)S(1)} %shard_map.73) | data formatting | bytes 65536 | tf_op jit(solution)/shard_map/reshape;transpose;reshape | solution.py:331

commit v2 on v1

--- a/solution.py
+++ b/solution.py
@@ -48,7 +48,7 @@
     mask_hbm, weight_hbm, slots_hbm, field_hbm, basis_hbm, gain_hbm, spectral_hbm,
     out_ref,
     mask_ref, weight_ref, slots_ref, slots_smem, field, basis, gain, spectral, table, filt, sent, held, lat_tab, left, mixed,
-    local_sem, filt_send, filt_recv, all_send, all_recv,
+    local_sem, filt_send, filt_recv, row_send, row_recv, band_send, band_recv,
 ):
     n_lat_dev, n_ord_dev, n_lat, n_lon, n_orders, channels, basis_count = dims
     lat_id = lax.axis_index("lat")
@@ -59,23 +59,23 @@
     per_slab = min(SLAB // 2, slots_here)
     width = 2 * per_slab
     groups = slots_here // per_slab
-    count = n_lat_dev * n_ord_dev
-    ord_mask = n_ord_dev - 1
-    ord_bits = log2(n_ord_dev)
     lat_rows = min(n_lat, COLUMNS // width)
     parts = n_lat // lat_rows
     cols = lat_rows * width
     out_rows = waves * width
 
-    def each_target(body):
-        if count <= 64:
-            for step in sorted(range(1, count), key=lambda step: (-(step & ord_mask), -step)):
-                body((lat_id ^ (step >> ord_bits), ord_id ^ (step & ord_mask)))
+    def steps(first, last, body):
+        if last - first <= 32:
+            for step in range(first, last):
+                body(step)
         else:
-            def one(step):
-                body((lat_id ^ (step >> ord_bits), ord_id ^ (step & ord_mask)))
-
-            pl.loop(1, count)(one)
+            pl.loop(first, last)(body)
+
+    def ord_peer(step):
+        return (lat_id, ord_id ^ step)
+
+    def lat_peer(step):
+        return (lat_id ^ step, ord_id)
 
     slots_copy = pltpu.make_async_copy(slots_hbm, slots_ref, local_sem.at[0])
     field_copy = pltpu.make_async_copy(field_hbm, field, local_sem.at[1])
@@ -87,6 +87,13 @@
     )
     spectral_copy = pltpu.make_async_copy(spectral_hbm, spectral, local_sem.at[6])
     basis_copy = pltpu.make_async_copy(basis_hbm, basis, local_sem.at[7])
+    barrier = pltpu.get_barrier_semaphore()
+
+    def greet(target):
+        pl.semaphore_signal(barrier, inc=1, device_id=target, device_id_type=MESH)
+
+    steps(1, n_ord_dev, lambda step: greet(ord_peer(n_ord_dev - step)))
+    steps(1, n_lat_dev, lambda step: greet(lat_peer(step)))
     slots_copy.start()
     field_copy.start()
     mask_copy.start()
@@ -95,13 +102,6 @@
     basis_copy.start()
     gain_copy.start()
     spectral_copy.start()
-
-    barrier = pltpu.get_barrier_semaphore()
-
-    def greet(target):
-        pl.semaphore_signal(barrier, inc=1, device_id=target, device_id_type=MESH)
-
-    each_target(greet)
 
     filt[0] = jnp.zeros((1, LANES), F32)
     filt[n_lat + 1] = jnp.zeros((1, LANES), F32)
@@ -143,22 +143,49 @@
 
     repeat(2 * n_orders // block_rows, transform)
 
-    pl.semaphore_wait(barrier, count - 1)
-
-    def send(target):
-        pltpu.make_async_remote_copy(
-            src_ref=filt.at[row_id + 1], dst_ref=filt.at[row_id + 1],
-            send_sem=filt_send.at[0], recv_sem=filt_recv.at[0],
+    pl.semaphore_wait(barrier, n_ord_dev - 1 + n_lat_dev - 1)
+    band = lat_id * n_ord_dev
+
+    def filt_copy(source, which, target):
+        return pltpu.make_async_remote_copy(
+            src_ref=source, dst_ref=source, send_sem=filt_send.at[which], recv_sem=filt_recv.at[which],
             device_id=target, device_id_type=MESH,
-        ).start()
+        )
+
+    def send(step):
+        target = ord_peer(step)
+        filt_copy(filt.at[pl.ds(row_id + 1, 1)], 0, target).start()
         pltpu.make_async_remote_copy(
             src_ref=sent.at[pl.ds(target[1] * groups, groups)], dst_ref=held.at[:, row_id],
-            send_sem=all_send.at[0], recv_sem=all_recv.at[0],
-            device_id=target, device_id_type=MESH,
+            send_sem=row_send.at[0], recv_sem=row_recv.at[step], device_id=target, device_id_type=MESH,
         ).start()
 
-    each_target(send)
+    steps(1, n_ord_dev, lambda step: send(n_ord_dev - step))
     held[:, row_id] = sent[pl.ds(ord_id * groups, groups)]
+
+    def row_arrival(step):
+        return pltpu.make_async_remote_copy(
+            src_ref=held.at[:, row_id], dst_ref=held.at[:, row_id],
+            send_sem=row_send.at[0], recv_sem=row_recv.at[step], device_id=ord_peer(1), device_id_type=MESH,
+        )
+
+    def band_copy(first, rows, target):
+        return pltpu.make_async_remote_copy(
+            src_ref=held.at[:, pl.ds(first, rows)], dst_ref=held.at[:, pl.ds(first, rows)],
+            send_sem=band_send.at[0], recv_sem=band_recv.at[0], device_id=target, device_id_type=MESH,
+        )
+
+    def hand_on(pair):
+        if not isinstance(pair, int) or pair > 0:
+            row_arrival(2 * pair).wait_recv()
+        row_arrival(2 * pair + 1).wait_recv()
+        first = band + 2 * ((ord_id >> 1) ^ pair)
+        steps(1, n_lat_dev, lambda step: band_copy(first, 2, lat_peer(n_lat_dev - step)).start())
+
+    hand_on(0)
+    filt_copy(filt.at[pl.ds(0, n_ord_dev - 1)], 0, ord_peer(1)).wait_recv()
+    steps(1, n_lat_dev, lambda step: filt_copy(filt.at[pl.ds(band + 1, n_ord_dev)], 1, lat_peer(n_lat_dev - step)).start())
+    steps(1, n_ord_dev // 2, hand_on)
 
     smem_copy.wait()
 
@@ -197,17 +224,8 @@
     gain_copy.wait()
     spectral_copy.wait()
     basis_copy.wait()
-    filt_arrivals = pltpu.make_async_remote_copy(
-        src_ref=filt.at[pl.ds(0, count - 1)], dst_ref=filt.at[pl.ds(0, count - 1)],
-        send_sem=filt_send.at[0], recv_sem=filt_recv.at[0],
-        device_id=(lat_id, ord_id ^ 1), device_id_type=MESH,
-    )
-    arrivals = pltpu.make_async_remote_copy(
-        src_ref=held.at[:, pl.ds(0, count - 1)], dst_ref=held.at[:, pl.ds(0, count - 1)],
-        send_sem=all_send.at[0], recv_sem=all_recv.at[0],
-        device_id=(lat_id, ord_id ^ 1), device_id_type=MESH,
-    )
-    filt_arrivals.wait_recv()
+    far_rows = (n_lat_dev - 1) * n_ord_dev
+    filt_copy(filt.at[pl.ds(0, far_rows)], 1, lat_peer(1)).wait_recv()
 
     def build_left(part, factors):
         window = filt[pl.ds(part * lat_rows, lat_rows + 2)].reshape(lat_rows + 2, LANES)
@@ -270,9 +288,15 @@
 
     if single_lat:
         build_left(0, factors)
+    arrivals = band_copy(0, far_rows, lat_peer(1))
     arrivals.wait_recv()
     repeat(groups, finish)
-    filt_arrivals.wait_send()
+    filt_copy(filt.at[pl.ds(0, n_ord_dev - 1)], 0, ord_peer(1)).wait_send()
+    filt_copy(filt.at[pl.ds(0, far_rows)], 1, lat_peer(1)).wait_send()
+    pltpu.make_async_remote_copy(
+        src_ref=held.at[:, pl.ds(0, n_ord_dev - 1)], dst_ref=held.at[:, pl.ds(0, n_ord_dev - 1)],
+        send_sem=row_send.at[0], recv_sem=row_recv.at[0], device_id=ord_peer(1), device_id_type=MESH,
+    ).wait_send()
     arrivals.wait_send()
 
 
@@ -318,8 +342,10 @@
             pltpu.VMEM((basis_count * out_rows, lat_rows * width), BF16),
             pltpu.VMEM((8, LANES) if single else (basis_count * out_rows, channels), F32),
             pltpu.SemaphoreType.DMA((8,)),
+            pltpu.SemaphoreType.DMA((2,)),
+            pltpu.SemaphoreType.DMA((2,)),
             pltpu.SemaphoreType.DMA((1,)),
-            pltpu.SemaphoreType.DMA((1,)),
+            pltpu.SemaphoreType.DMA((n_ord_dev,)),
             pltpu.SemaphoreType.DMA((1,)),
             pltpu.SemaphoreType.DMA((1,)),
         ],

time: 13.6 us -> 13.8 us (1.015)
  Pallas kernels: 12.8 us -> 13 us
    pallas_call x1, Pallas kernels: 12.8 us -> 13 us  [per_device(): pl.pallas_call(functools.partial(kernel, dims), out_shape=pltpu.VMEM((gro...]
where the time goes in v2:
time: 13.8 us; the launch traced here: 13.7 us
  Pallas kernels  13 us (94%)
  local copies, waits for them, and re-layouts  0.63 us (5%)
    pallas_call x1, Pallas kernels, per_device(): pl.pallas_call(functools.partial(kernel, dims), out_shape=pltpu.VMEM((gro...  13 us
    another operation x1, local copies, waits for them, and re-layouts, per_device(): return jnp.swapaxes(result, 0, 1).reshape(waves, slots_here, 2, channels)  0.63 us

profile of v2, /device:TPU:0, one launch (start us, length us, event | category | flops | bytes accessed | tf_op | source)
XLA Modules:
  0.0 13.7 jit_solution(7418629821907824309)
XLA Ops:
  0.0 13.0 %shard_map.73 = bf16[1,64,256]{2,1,0:T(8,128)(2,1)S(1)} custom-call(s32[1,8,15]{2,1,0:T(8,128)} %mask_hbm.1, f32[1,8,15]{2,1,0:T(8,128)} %weight_hbm.1, s32[1,32]{1,0:T(1,128)} %bitcast.1, bf16[1,64,256]{2,1,0:T(8,128)(2,1)} %field_hbm.1, bf16[8,256,256]{2,1,0:T(8,128)(2,1)} %basis_hbm.1, f32[32,256]{1,0:T(8,128)} %gain_hbm.1, bf16[2,256,256]{2,1,0:T(8,128)(2,1)} %spectral_hbm.1), custom_call_target="tpu_custom_call" | custom-call | tf_op jit(solution)/shard_map/pallas_call | solution.py:323
  13.0 0.6 %reshape_transpose_reshape.3 = bf16[8,4,2,256]{3,2,1,0:T(2,128)(2,1)} reshape(bf16[1,64,256]{2,1,0:T(8,128)(2,1)S(1)} %shard_map.73) | data formatting | bytes 65536 | tf_op jit(solution)/shard_map/reshape;transpose;reshape | solution.py:357

commit v3 on v1

--- a/solution.py
+++ b/solution.py
@@ -48,7 +48,7 @@
     mask_hbm, weight_hbm, slots_hbm, field_hbm, basis_hbm, gain_hbm, spectral_hbm,
     out_ref,
     mask_ref, weight_ref, slots_ref, slots_smem, field, basis, gain, spectral, table, filt, sent, held, lat_tab, left, mixed,
-    local_sem, filt_send, filt_recv, all_send, all_recv,
+    local_sem, filt_send, filt_recv, all_send, all_recv, ready,
 ):
     n_lat_dev, n_ord_dev, n_lat, n_lon, n_orders, channels, basis_count = dims
     lat_id = lax.axis_index("lat")
@@ -60,22 +60,17 @@
     width = 2 * per_slab
     groups = slots_here // per_slab
     count = n_lat_dev * n_ord_dev
-    ord_mask = n_ord_dev - 1
-    ord_bits = log2(n_ord_dev)
     lat_rows = min(n_lat, COLUMNS // width)
     parts = n_lat // lat_rows
     cols = lat_rows * width
     out_rows = waves * width
 
-    def each_target(body):
-        if count <= 64:
-            for step in sorted(range(1, count), key=lambda step: (-(step & ord_mask), -step)):
-                body((lat_id ^ (step >> ord_bits), ord_id ^ (step & ord_mask)))
-        else:
-            def one(step):
-                body((lat_id ^ (step >> ord_bits), ord_id ^ (step & ord_mask)))
-
-            pl.loop(1, count)(one)
+    lat_bits = log2(n_lat_dev)
+    rank = ((ord_id >> 1) * n_lat_dev + lat_id) * 2 + 1 - (ord_id & 1)
+    per_ready = 1 if count <= 64 else 32
+
+    def device(other):
+        return ((other >> 1) & (n_lat_dev - 1), ((other >> (1 + lat_bits)) << 1) + 1 - (other & 1))
 
     slots_copy = pltpu.make_async_copy(slots_hbm, slots_ref, local_sem.at[0])
     field_copy = pltpu.make_async_copy(field_hbm, field, local_sem.at[1])
@@ -91,17 +86,16 @@
     field_copy.start()
     mask_copy.start()
     weight_copy.start()
+    barrier = pltpu.get_barrier_semaphore()
+
+    def greet(other):
+        pl.semaphore_signal(barrier, inc=1, device_id=device(other), device_id_type=MESH)
+
+    pl.loop(rank + 1, count)(greet)
     smem_copy.start()
     basis_copy.start()
     gain_copy.start()
     spectral_copy.start()
-
-    barrier = pltpu.get_barrier_semaphore()
-
-    def greet(target):
-        pl.semaphore_signal(barrier, inc=1, device_id=target, device_id_type=MESH)
-
-    each_target(greet)
 
     filt[0] = jnp.zeros((1, LANES), F32)
     filt[n_lat + 1] = jnp.zeros((1, LANES), F32)
@@ -133,6 +127,14 @@
     spread = jnp.where(lane % basis_count == iota((basis_count, LANES), 0), spread, 0.0)
     filt[row_id + 1] = jnp.sum(spread, axis=0, keepdims=True)
 
+    @pl.when(rank > 0)
+    def _():
+        pl.semaphore_wait(barrier, rank)
+
+    def call(other):
+        pl.semaphore_signal(ready.at[rank // per_ready], inc=1, device_id=device(other), device_id_type=MESH)
+
+    pl.loop(0, rank)(call)
     field_copy.wait()
 
     def transform(block):
@@ -143,9 +145,8 @@
 
     repeat(2 * n_orders // block_rows, transform)
 
-    pl.semaphore_wait(barrier, count - 1)
-
-    def send(target):
+    def send(other):
+        target = device(other)
         pltpu.make_async_remote_copy(
             src_ref=filt.at[row_id + 1], dst_ref=filt.at[row_id + 1],
             send_sem=filt_send.at[0], recv_sem=filt_recv.at[0],
@@ -157,7 +158,7 @@
             device_id=target, device_id_type=MESH,
         ).start()
 
-    each_target(send)
+    pl.loop(0, rank)(send)
     held[:, row_id] = sent[pl.ds(ord_id * groups, groups)]
 
     smem_copy.wait()
@@ -194,6 +195,13 @@
         lat_tables(0, 0)
         factors = tap_factors(0)
 
+    def answer(block):
+        first = jnp.maximum(rank + 1, block * per_ready)
+        last = (block + 1) * per_ready
+        pl.semaphore_wait(ready.at[block], last - first)
+        pl.loop(first, last)(send)
+
+    pl.loop((rank + 1) // per_ready, count // per_ready)(answer)
     gain_copy.wait()
     spectral_copy.wait()
     basis_copy.wait()
@@ -322,6 +330,7 @@
             pltpu.SemaphoreType.DMA((1,)),
             pltpu.SemaphoreType.DMA((1,)),
             pltpu.SemaphoreType.DMA((1,)),
+            pltpu.SemaphoreType.REGULAR((max(1, n_lat // (1 if n_lat <= 64 else 32)),)),
         ],
         compiler_params=pltpu.CompilerParams(
             collective_id=0, has_side_effects=True, vmem_limit_bytes=63 * 1024 * 1024

time: 13.6 us -> 12.2 us (0.90)
  Pallas kernels: 12.8 us -> 11.4 us
    pallas_call x1, Pallas kernels: 12.8 us -> 11.4 us  [per_device(): pl.pallas_call(functools.partial(kernel, dims), out_shape=pltpu.VMEM((gro...]
where the time goes in v3:
time: 12.2 us; the launch traced here: 12.1 us
  Pallas kernels  11.4 us (93%)
  local copies, waits for them, and re-layouts  0.63 us (5%)
    pallas_call x1, Pallas kernels, per_device(): pl.pallas_call(functools.partial(kernel, dims), out_shape=pltpu.VMEM((gro...  11.4 us
    another operation x1, local copies, waits for them, and re-layouts, per_device(): return jnp.swapaxes(result, 0, 1).reshape(waves, slots_here, 2, channels)  0.63 us

profile of v3, /device:TPU:0, one launch (start us, length us, event | category | flops | bytes accessed | tf_op | source)
XLA Modules:
  0.0 12.1 jit_solution(1635578268668769523)
XLA Ops:
  0.0 11.4 %shard_map.73 = bf16[1,64,256]{2,1,0:T(8,128)(2,1)S(1)} custom-call(s32[1,8,15]{2,1,0:T(8,128)} %mask_hbm.1, f32[1,8,15]{2,1,0:T(8,128)} %weight_hbm.1, s32[1,32]{1,0:T(1,128)} %bitcast.1, bf16[1,64,256]{2,1,0:T(8,128)(2,1)} %field_hbm.1, bf16[8,256,256]{2,1,0:T(8,128)(2,1)} %basis_hbm.1, f32[32,256]{1,0:T(8,128)} %gain_hbm.1, bf16[2,256,256]{2,1,0:T(8,128)(2,1)} %spectral_hbm.1), custom_call_target="tpu_custom_call" | custom-call | tf_op jit(solution)/shard_map/pallas_call | solution.py:307
  11.4 0.6 %reshape_transpose_reshape.3 = bf16[8,4,2,256]{3,2,1,0:T(2,128)(2,1)} reshape(bf16[1,64,256]{2,1,0:T(8,128)(2,1)S(1)} %shard_map.73) | data formatting | bytes 65536 | tf_op jit(solution)/shard_map/reshape;transpose;reshape | solution.py:340

commit v4 on v3

--- a/solution.py
+++ b/solution.py
@@ -82,16 +82,16 @@
     )
     spectral_copy = pltpu.make_async_copy(spectral_hbm, spectral, local_sem.at[6])
     basis_copy = pltpu.make_async_copy(basis_hbm, basis, local_sem.at[7])
+    barrier = pltpu.get_barrier_semaphore()
+
+    def greet(other):
+        pl.semaphore_signal(barrier, inc=1, device_id=device(other), device_id_type=MESH)
+
+    pl.loop(rank + 1, count)(greet)
     slots_copy.start()
     field_copy.start()
     mask_copy.start()
     weight_copy.start()
-    barrier = pltpu.get_barrier_semaphore()
-
-    def greet(other):
-        pl.semaphore_signal(barrier, inc=1, device_id=device(other), device_id_type=MESH)
-
-    pl.loop(rank + 1, count)(greet)
     smem_copy.start()
     basis_copy.start()
     gain_copy.start()
@@ -127,14 +127,6 @@
     spread = jnp.where(lane % basis_count == iota((basis_count, LANES), 0), spread, 0.0)
     filt[row_id + 1] = jnp.sum(spread, axis=0, keepdims=True)
 
-    @pl.when(rank > 0)
-    def _():
-        pl.semaphore_wait(barrier, rank)
-
-    def call(other):
-        pl.semaphore_signal(ready.at[rank // per_ready], inc=1, device_id=device(other), device_id_type=MESH)
-
-    pl.loop(0, rank)(call)
     field_copy.wait()
 
     def transform(block):
@@ -158,7 +150,16 @@
             device_id=target, device_id_type=MESH,
         ).start()
 
-    pl.loop(0, rank)(send)
+    def call(other):
+        pl.semaphore_signal(ready.at[rank // per_ready], inc=1, device_id=device(other), device_id_type=MESH)
+
+    @pl.when(rank > 0)
+    def _():
+        pl.semaphore_wait(barrier, rank)
+
+    pl.loop(0, jnp.minimum(rank, 2))(send)
+    pl.loop(0, rank)(call)
+    pl.loop(jnp.minimum(rank, 2), rank)(send)
     held[:, row_id] = sent[pl.ds(ord_id * groups, groups)]
 
     smem_copy.wait()

time: 12.2 us -> 11.8 us (0.967)
  Pallas kernels: 11.4 us -> 11 us
    pallas_call x1, Pallas kernels: 11.4 us -> 11 us  [per_device(): pl.pallas_call(functools.partial(kernel, dims), out_shape=pltpu.VMEM((gro...]
where the time goes in v4:
time: 11.8 us; the launch traced here: 11.6 us
  Pallas kernels  11 us (93%)
  local copies, waits for them, and re-layouts  0.63 us (5%)
    pallas_call x1, Pallas kernels, per_device(): pl.pallas_call(functools.partial(kernel, dims), out_shape=pltpu.VMEM((gro...  11 us
    another operation x1, local copies, waits for them, and re-layouts, per_device(): return jnp.swapaxes(result, 0, 1).reshape(waves, slots_here, 2, channels)  0.63 us

profile of v4, /device:TPU:0, one launch (start us, length us, event | category | flops | bytes accessed | tf_op | source)
XLA Modules:
  0.0 11.6 jit_solution(17817632520189517982)
XLA Ops:
  0.0 11.0 %shard_map.73 = bf16[1,64,256]{2,1,0:T(8,128)(2,1)S(1)} custom-call(s32[1,8,15]{2,1,0:T(8,128)} %mask_hbm.1, f32[1,8,15]{2,1,0:T(8,128)} %weight_hbm.1, s32[1,32]{1,0:T(1,128)} %bitcast.1, bf16[1,64,256]{2,1,0:T(8,128)(2,1)} %field_hbm.1, bf16[8,256,256]{2,1,0:T(8,128)(2,1)} %basis_hbm.1, f32[32,256]{1,0:T(8,128)} %gain_hbm.1, bf16[2,256,256]{2,1,0:T(8,128)(2,1)} %spectral_hbm.1), custom_call_target="tpu_custom_call" | custom-call | tf_op jit(solution)/shard_map/pallas_call | solution.py:308
  11.0 0.6 %reshape_transpose_reshape.3 = bf16[8,4,2,256]{3,2,1,0:T(2,128)(2,1)} reshape(bf16[1,64,256]{2,1,0:T(8,128)(2,1)S(1)} %shard_map.73) | data formatting | bytes 65536 | tf_op jit(solution)/shard_map/reshape;transpose;reshape | solution.py:341

commit v5 on v4

--- a/solution.py
+++ b/solution.py
@@ -66,11 +66,25 @@
     out_rows = waves * width
 
     lat_bits = log2(n_lat_dev)
-    rank = ((ord_id >> 1) * n_lat_dev + lat_id) * 2 + 1 - (ord_id & 1)
-    per_ready = 1 if count <= 64 else 32
-
-    def device(other):
-        return ((other >> 1) & (n_lat_dev - 1), ((other >> (1 + lat_bits)) << 1) + 1 - (other & 1))
+    lat_mask = n_lat_dev - 1
+    levels = n_ord_dev // 2
+    chips = levels * n_lat_dev
+    level = ord_id >> 1
+    chip = level * n_lat_dev + lat_id
+    leader = (ord_id & 1) == 1
+    follower = (ord_id & 1) == 0
+    half = levels // 2
+    top = (levels - 1) * n_lat_dev
+    low = level < half
+    sibling = (lat_id, ord_id ^ 1)
+    per_ready = 1 if chips <= 64 else n_lat_dev
+
+    def device(other, core):
+        return (other & lat_mask, ((other >> lat_bits) << 1) + core)
+
+    def on_both(other, body):
+        body(device(other, 0))
+        body(device(other, 1))
 
     slots_copy = pltpu.make_async_copy(slots_hbm, slots_ref, local_sem.at[0])
     field_copy = pltpu.make_async_copy(field_hbm, field, local_sem.at[1])
@@ -84,10 +98,23 @@
     basis_copy = pltpu.make_async_copy(basis_hbm, basis, local_sem.at[7])
     barrier = pltpu.get_barrier_semaphore()
 
-    def greet(other):
-        pl.semaphore_signal(barrier, inc=1, device_id=device(other), device_id_type=MESH)
-
-    pl.loop(rank + 1, count)(greet)
+    def greet(target):
+        pl.semaphore_signal(barrier, inc=1, device_id=target, device_id_type=MESH)
+
+    def signal(semaphore, target):
+        pl.semaphore_signal(semaphore, inc=1, device_id=target, device_id_type=MESH)
+
+    greet(sibling)
+    pl.loop(chip + 1, chips)(lambda other: greet(device(other, 1)))
+
+    @pl.when(chip == 0)
+    def _():
+        pl.loop(half * n_lat_dev, chips)(lambda other: greet(device(other, 0)))
+
+    @pl.when(level == levels - 1)
+    def _():
+        pl.loop(0, half * n_lat_dev)(lambda other: greet(device(other, 0)))
+
     slots_copy.start()
     field_copy.start()
     mask_copy.start()
@@ -127,6 +154,39 @@
     spread = jnp.where(lane % basis_count == iota((basis_count, LANES), 0), spread, 0.0)
     filt[row_id + 1] = jnp.sum(spread, axis=0, keepdims=True)
 
+    def send_filters(target):
+        pltpu.make_async_remote_copy(
+            src_ref=filt.at[row_id + 1], dst_ref=filt.at[row_id + 1],
+            send_sem=filt_send.at[0], recv_sem=filt_recv.at[0],
+            device_id=target, device_id_type=MESH,
+        ).start()
+
+    def send_rows(target):
+        pltpu.make_async_remote_copy(
+            src_ref=sent.at[pl.ds(target[1] * groups, groups)], dst_ref=held.at[:, row_id],
+            send_sem=all_send.at[0], recv_sem=all_recv.at[0],
+            device_id=target, device_id_type=MESH,
+        ).start()
+
+    def send(target):
+        send_filters(target)
+        send_rows(target)
+
+    early_sem, known_sem, top_sem = ready.at[chips // per_ready], ready.at[chips // per_ready + 1], ready.at[chips // per_ready + 2]
+
+    @pl.when(jnp.logical_and(follower, jnp.logical_not(low)))
+    def _():
+        pl.semaphore_wait(barrier, 3)
+        signal(early_sem, sibling)
+
+    @pl.when(jnp.logical_and(leader, jnp.logical_not(low)))
+    def _():
+        pl.semaphore_wait(early_sem, 1)
+
+    @pl.when(jnp.logical_not(low))
+    def _():
+        on_both(0, send_filters)
+
     field_copy.wait()
 
     def transform(block):
@@ -137,29 +197,24 @@
 
     repeat(2 * n_orders // block_rows, transform)
 
-    def send(other):
-        target = device(other)
-        pltpu.make_async_remote_copy(
-            src_ref=filt.at[row_id + 1], dst_ref=filt.at[row_id + 1],
-            send_sem=filt_send.at[0], recv_sem=filt_recv.at[0],
-            device_id=target, device_id_type=MESH,
-        ).start()
-        pltpu.make_async_remote_copy(
-            src_ref=sent.at[pl.ds(target[1] * groups, groups)], dst_ref=held.at[:, row_id],
-            send_sem=all_send.at[0], recv_sem=all_recv.at[0],
-            device_id=target, device_id_type=MESH,
-        ).start()
-
-    def call(other):
-        pl.semaphore_signal(ready.at[rank // per_ready], inc=1, device_id=device(other), device_id_type=MESH)
-
-    @pl.when(rank > 0)
-    def _():
-        pl.semaphore_wait(barrier, rank)
-
-    pl.loop(0, jnp.minimum(rank, 2))(send)
-    pl.loop(0, rank)(call)
-    pl.loop(jnp.minimum(rank, 2), rank)(send)
+    @pl.when(jnp.logical_not(low))
+    def _():
+        on_both(0, send_rows)
+
+    @pl.when(leader)
+    def _():
+        pl.semaphore_wait(barrier, 2 * chip + 1)
+        signal(known_sem, sibling)
+        block = chip // per_ready
+        first = jnp.where(level == levels - 1, half * n_lat_dev, 0)
+        pl.loop(first, chip)(lambda other: on_both(other, lambda target: signal(ready.at[block], target)))
+
+    @pl.when(follower)
+    def _():
+        pl.semaphore_wait(known_sem, 1)
+
+    pl.loop(jnp.where(low, 0, 1), chip)(lambda other: on_both(other, send))
+    send(sibling)
     held[:, row_id] = sent[pl.ds(ord_id * groups, groups)]
 
     smem_copy.wait()
@@ -197,12 +252,46 @@
         factors = tap_factors(0)
 
     def answer(block):
-        first = jnp.maximum(rank + 1, block * per_ready)
+        first = jnp.maximum(chip + 1, block * per_ready)
         last = (block + 1) * per_ready
-        pl.semaphore_wait(ready.at[block], last - first)
-        pl.loop(first, last)(send)
-
-    pl.loop((rank + 1) // per_ready, count // per_ready)(answer)
+
+        @pl.when(jnp.logical_or(jnp.logical_not(low), block < top // per_ready))
+        def _():
+            pl.semaphore_wait(ready.at[block], last - first)
+
+        pl.loop(first, last)(lambda other: on_both(other, send))
+
+    start = (chip + 1) // per_ready
+    half_block, top_block = half * n_lat_dev // per_ready, top // per_ready
+    pl.loop(start, half_block)(answer)
+
+    def answer_top():
+        pl.loop(jnp.maximum(start, top_block), chips // per_ready)(answer)
+
+    def answer_rest():
+        pl.loop(jnp.maximum(start, half_block), top_block)(answer)
+
+    top_first = jnp.logical_and(low, follower)
+
+    @pl.when(jnp.logical_not(top_first))
+    def _():
+        answer_rest()
+
+    @pl.when(jnp.logical_and(follower, low))
+    def _():
+        pl.semaphore_wait(barrier, 2 * n_lat_dev + 1)
+        signal(top_sem, sibling)
+
+    @pl.when(jnp.logical_and(leader, low))
+    def _():
+        pl.semaphore_wait(top_sem, 1)
+
+    answer_top()
+
+    @pl.when(top_first)
+    def _():
+        answer_rest()
+
     gain_copy.wait()
     spectral_copy.wait()
     basis_copy.wait()
@@ -331,7 +420,7 @@
             pltpu.SemaphoreType.DMA((1,)),
             pltpu.SemaphoreType.DMA((1,)),
             pltpu.SemaphoreType.DMA((1,)),
-            pltpu.SemaphoreType.REGULAR((max(1, n_lat // (1 if n_lat <= 64 else 32)),)),
+            pltpu.SemaphoreType.REGULAR((3 + n_lat // 2 // (1 if n_lat <= 128 else n_lat_dev),)),
         ],
         compiler_params=pltpu.CompilerParams(
             collective_id=0, has_side_effects=True, vmem_limit_bytes=63 * 1024 * 1024

time: 11.8 us -> 11.5 us (0.975)
  Pallas kernels: 11 us -> 10.7 us
    pallas_call x1, Pallas kernels: 11 us -> 10.7 us  [per_device(): pl.pallas_call(functools.partial(kernel, dims), out_shape=pltpu.VMEM((gro...]
where the time goes in v5:
time: 11.5 us; the launch traced here: 11.3 us
  Pallas kernels  10.7 us (93%)
  local copies, waits for them, and re-layouts  0.63 us (5%)
    pallas_call x1, Pallas kernels, per_device(): pl.pallas_call(functools.partial(kernel, dims), out_shape=pltpu.VMEM((gro...  10.7 us
    another operation x1, local copies, waits for them, and re-layouts, per_device(): return jnp.swapaxes(result, 0, 1).reshape(waves, slots_here, 2, channels)  0.63 us

profile of v5, /device:TPU:0, one launch (start us, length us, event | category | flops | bytes accessed | tf_op | source)
XLA Modules:
  0.0 11.3 jit_solution(7787838562862764489)
XLA Ops:
  0.0 10.7 %shard_map.73 = bf16[1,64,256]{2,1,0:T(8,128)(2,1)S(1)} custom-call(s32[1,8,15]{2,1,0:T(8,128)} %mask_hbm.1, f32[1,8,15]{2,1,0:T(8,128)} %weight_hbm.1, s32[1,32]{1,0:T(1,128)} %bitcast.1, bf16[1,64,256]{2,1,0:T(8,128)(2,1)} %field_hbm.1, bf16[8,256,256]{2,1,0:T(8,128)(2,1)} %basis_hbm.1, f32[32,256]{1,0:T(8,128)} %gain_hbm.1, bf16[2,256,256]{2,1,0:T(8,128)(2,1)} %spectral_hbm.1), custom_call_target="tpu_custom_call" | custom-call | tf_op jit(solution)/shard_map/pallas_call | solution.py:397
  10.7 0.6 %reshape_transpose_reshape.3 = bf16[8,4,2,256]{3,2,1,0:T(2,128)(2,1)} reshape(bf16[1,64,256]{2,1,0:T(8,128)(2,1)S(1)} %shard_map.73) | data formatting | bytes 65536 | tf_op jit(solution)/shard_map/reshape;transpose;reshape | solution.py:430

commit v6 on v5

--- a/solution.py
+++ b/solution.py
@@ -83,8 +83,8 @@
         return (other & lat_mask, ((other >> lat_bits) << 1) + core)
 
     def on_both(other, body):
+        body(device(other, 1))
         body(device(other, 0))
-        body(device(other, 1))
 
     slots_copy = pltpu.make_async_copy(slots_hbm, slots_ref, local_sem.at[0])
     field_copy = pltpu.make_async_copy(field_hbm, field, local_sem.at[1])
@@ -104,6 +104,10 @@
     def signal(semaphore, target):
         pl.semaphore_signal(semaphore, inc=1, device_id=target, device_id_type=MESH)
 
+    mask_copy.start()
+    weight_copy.start()
+    slots_copy.start()
+    field_copy.start()
     greet(sibling)
     pl.loop(chip + 1, chips)(lambda other: greet(device(other, 1)))
 
@@ -115,33 +119,13 @@
     def _():
         pl.loop(0, half * n_lat_dev)(lambda other: greet(device(other, 0)))
 
-    slots_copy.start()
-    field_copy.start()
-    mask_copy.start()
-    weight_copy.start()
     smem_copy.start()
     basis_copy.start()
     gain_copy.start()
     spectral_copy.start()
 
-    filt[0] = jnp.zeros((1, LANES), F32)
-    filt[n_lat + 1] = jnp.zeros((1, LANES), F32)
-
-    slots_copy.wait()
-    orders = slots_ref[...]
-    block_rows = table.shape[0]
-
-    def dft_block(start):
-        row = iota((block_rows, 1), 0) + start
-        found = iota((block_rows, n_orders), 1) == row >> 1
-        order = jnp.sum(jnp.where(found, orders.astype(F32), 0.0), axis=1, keepdims=True).astype(jnp.int32)
-        phase = order * iota((block_rows, n_lon), 1) + (n_lon // 4) * (row & 1)
-        table[...] = (cosine(phase, n_lon) * (1.0 / math.sqrt(n_lon))).astype(BF16)
-
-    single_dft = block_rows == 2 * n_orders
-    if single_dft:
-        dft_block(0)
-    slabs = block_rows // width
+    filt[pl.ds(0, 1)] = jnp.zeros((1, LANES), F32)
+    filt[pl.ds(n_lat + 1, 1)] = jnp.zeros((1, LANES), F32)
 
     mask_copy.wait()
     weight_copy.wait()
@@ -152,11 +136,11 @@
     for tap in range(tap_count):
         spread = jnp.where(lane // basis_count == tap, taps[:, tap:tap + 1], spread)
     spread = jnp.where(lane % basis_count == iota((basis_count, LANES), 0), spread, 0.0)
-    filt[row_id + 1] = jnp.sum(spread, axis=0, keepdims=True)
+    filt[pl.ds(row_id + 1, 1)] = jnp.sum(spread, axis=0, keepdims=True)
 
     def send_filters(target):
         pltpu.make_async_remote_copy(
-            src_ref=filt.at[row_id + 1], dst_ref=filt.at[row_id + 1],
+            src_ref=filt.at[pl.ds(row_id + 1, 1)], dst_ref=filt.at[pl.ds(row_id + 1, 1)],
             send_sem=filt_send.at[0], recv_sem=filt_recv.at[0],
             device_id=target, device_id_type=MESH,
         ).start()
@@ -185,7 +169,24 @@
 
     @pl.when(jnp.logical_not(low))
     def _():
-        on_both(0, send_filters)
+        send_filters(device(0, 0))
+        send_filters(device(0, 1))
+
+    slots_copy.wait()
+    orders = slots_ref[...]
+    block_rows = table.shape[0]
+
+    def dft_block(start):
+        row = iota((block_rows, 1), 0) + start
+        found = iota((block_rows, n_orders), 1) == row >> 1
+        order = jnp.sum(jnp.where(found, orders.astype(F32), 0.0), axis=1, keepdims=True).astype(jnp.int32)
+        phase = order * iota((block_rows, n_lon), 1) + (n_lon // 4) * (row & 1)
+        table[...] = (cosine(phase, n_lon) * (1.0 / math.sqrt(n_lon))).astype(BF16)
+
+    single_dft = block_rows == 2 * n_orders
+    if single_dft:
+        dft_block(0)
+    slabs = block_rows // width
 
     field_copy.wait()
 
@@ -199,7 +200,8 @@
 
     @pl.when(jnp.logical_not(low))
     def _():
-        on_both(0, send_rows)
+        send_rows(device(0, 0))
+        send_rows(device(0, 1))
 
     @pl.when(leader)
     def _():
@@ -308,7 +310,7 @@
     filt_arrivals.wait_recv()
 
     def build_left(part, factors):
-        window = filt[pl.ds(part * lat_rows, lat_rows + 2)].reshape(lat_rows + 2, LANES)
+        window = filt[pl.ds(part * lat_rows, lat_rows + 2)]
         high = window.astype(BF16)
         low = (window - high.astype(F32)).astype(BF16)
         both = jnp.concatenate([high.astype(F32), low.astype(F32)], axis=0).T.astype(BF16)
@@ -409,7 +411,7 @@
             pltpu.VMEM((waves, channels), F32),
             pltpu.VMEM((2, channels, channels), BF16),
             pltpu.VMEM((block_rows, n_lon), BF16),
-            pltpu.VMEM((n_lat + 2, 1, LANES), F32),
+            pltpu.VMEM((n_lat + 2, LANES), F32),
             pltpu.VMEM((n_ord_dev * groups, width, channels), BF16),
             pltpu.VMEM((groups, n_lat, width, channels), BF16),
             pltpu.VMEM((3, out_rows, lat_rows * width), F32),

time: 11.5 us -> 11.4 us (level)
  no operation moved by 1% of the time
where the time goes in v6:
time: 11.4 us; the launch traced here: 11.2 us
  Pallas kernels  10.6 us (93%)
  local copies, waits for them, and re-layouts  0.63 us (6%)
    pallas_call x1, Pallas kernels, per_device(): pl.pallas_call(functools.partial(kernel, dims), out_shape=pltpu.VMEM((gro...  10.6 us
    another operation x1, local copies, waits for them, and re-layouts, per_device(): return jnp.swapaxes(result, 0, 1).reshape(waves, slots_here, 2, channels)  0.63 us

profile of v6, /device:TPU:0, one launch (start us, length us, event | category | flops | bytes accessed | tf_op | source)
XLA Modules:
  0.0 11.2 jit_solution(12464248785070502195)
XLA Ops:
  0.0 10.6 %shard_map.73 = bf16[1,64,256]{2,1,0:T(8,128)(2,1)S(1)} custom-call(s32[1,8,15]{2,1,0:T(8,128)} %mask_hbm.1, f32[1,8,15]{2,1,0:T(8,128)} %weight_hbm.1, s32[1,32]{1,0:T(1,128)} %bitcast.1, bf16[1,64,256]{2,1,0:T(8,128)(2,1)} %field_hbm.1, bf16[8,256,256]{2,1,0:T(8,128)(2,1)} %basis_hbm.1, f32[32,256]{1,0:T(8,128)} %gain_hbm.1, bf16[2,256,256]{2,1,0:T(8,128)(2,1)} %spectral_hbm.1), custom_call_target="tpu_custom_call" | custom-call | tf_op jit(solution)/shard_map/pallas_call | solution.py:399
  10.6 0.6 %reshape_transpose_reshape.3 = bf16[8,4,2,256]{3,2,1,0:T(2,128)(2,1)} reshape(bf16[1,64,256]{2,1,0:T(8,128)(2,1)S(1)} %shard_map.73) | data formatting | bytes 65536 | tf_op jit(solution)/shard_map/reshape;transpose;reshape | solution.py:432

commit v7 on v6

--- a/solution.py
+++ b/solution.py
@@ -47,7 +47,7 @@
     dims,
     mask_hbm, weight_hbm, slots_hbm, field_hbm, basis_hbm, gain_hbm, spectral_hbm,
     out_ref,
-    mask_ref, weight_ref, slots_ref, slots_smem, field, basis, gain, spectral, table, filt, sent, held, lat_tab, left, mixed,
+    mask_ref, weight_ref, slots_ref, slots_smem, field, basis, gain, spectral, table, filt, sent, held, lat_tab, select, left, mixed,
     local_sem, filt_send, filt_recv, all_send, all_recv, ready,
 ):
     n_lat_dev, n_ord_dev, n_lat, n_lon, n_orders, channels, basis_count = dims
@@ -196,12 +196,24 @@
         rows = jnp.dot(table[...], field[0], preferred_element_type=F32).astype(BF16)
         sent[pl.ds(block * slabs, slabs)] = rows.reshape(slabs, width, channels)
 
-    repeat(2 * n_orders // block_rows, transform)
-
-    @pl.when(jnp.logical_not(low))
-    def _():
-        send_rows(device(0, 0))
-        send_rows(device(0, 1))
+    def send_first():
+        @pl.when(jnp.logical_not(low))
+        def _():
+            send_rows(device(0, 0))
+            send_rows(device(0, 1))
+
+    def transform_rows(first, last):
+        rows = jnp.dot(table[first:last], field[0], preferred_element_type=F32).astype(BF16)
+        sent[first // width:last // width] = rows.reshape((last - first) // width, width, channels)
+
+    first_rows = 4 * slots_here
+    if single_dft and first_rows % 16 == 0 and first_rows < block_rows:
+        transform_rows(0, first_rows)
+        send_first()
+        transform_rows(first_rows, block_rows)
+    else:
+        repeat(2 * n_orders // block_rows, transform)
+        send_first()
 
     @pl.when(leader)
     def _():
@@ -247,6 +259,12 @@
         part_of = iota((16, cols), 1) & 1
         phase = order * lon_step + (n_lon // 4) * (part_of - (row >> 3))
         return cosine(phase, n_lon)
+
+    window_row = iota((lat_rows + 2, cols), 0)
+    window_lat = iota((lat_rows + 2, cols), 1) >> log2(width)
+    for step in range(3):
+        chosen = (window_row == window_lat + 2 - step).astype(F32)
+        select[step] = jnp.concatenate([chosen, chosen], axis=0).astype(BF16)
 
     single_lat = groups == 1 and parts == 1
     if single_lat:
@@ -314,14 +332,10 @@
         high = window.astype(BF16)
         low = (window - high.astype(F32)).astype(BF16)
         both = jnp.concatenate([high.astype(F32), low.astype(F32)], axis=0).T.astype(BF16)
-        row = iota((lat_rows + 2, cols), 0)
-        lat = iota((lat_rows + 2, cols), 1) >> log2(width)
         real, imag = [], []
         for step in range(3):
-            chosen = (row == lat + 2 - step).astype(F32)
-            chosen = jnp.concatenate([chosen, chosen], axis=0).astype(BF16)
             first = 5 * step * basis_count
-            wide = jnp.dot(both[first:first + 5 * basis_count], chosen, preferred_element_type=F32)
+            wide = jnp.dot(both[first:first + 5 * basis_count], select[step], preferred_element_type=F32)
             sums = [None, None]
             for lon_step in range(5):
                 values = wide[lon_step * basis_count:(lon_step + 1) * basis_count]
@@ -359,7 +373,11 @@
             total = mixed[...]
         total = total.astype(BF16)
         flat = jnp.concatenate([total[b * out_rows:(b + 1) * out_rows] for b in range(basis_count)], axis=1)
-        coefficients = jnp.dot(flat, basis[...].reshape(basis_count * channels, channels), preferred_element_type=F32)
+        weights = basis[...].reshape(basis_count * channels, channels)
+        coefficients = jnp.concatenate(
+            [jnp.dot(flat, weights[:, first:first + LANES], preferred_element_type=F32) for first in range(0, channels, LANES)],
+            axis=1,
+        )
         scaled = (coefficients.reshape(waves, width, channels) * gain[...][:, None, :]).astype(BF16)
         scaled = scaled.reshape(out_rows, channels)
         straight = jnp.dot(scaled, spectral[0], preferred_element_type=F32)
@@ -415,6 +433,7 @@
             pltpu.VMEM((n_ord_dev * groups, width, channels), BF16),
             pltpu.VMEM((groups, n_lat, width, channels), BF16),
             pltpu.VMEM((3, out_rows, lat_rows * width), F32),
+            pltpu.VMEM((3, 2 * (lat_rows + 2), lat_rows * width), BF16),
             pltpu.VMEM((basis_count * out_rows, lat_rows * width), BF16),
             pltpu.VMEM((8, LANES) if single else (basis_count * out_rows, channels), F32),
             pltpu.SemaphoreType.DMA((8,)),

time: 11.4 us -> 11.3 us (level)
  no operation moved by 1% of the time
where the time goes in v7:
time: 11.3 us; the launch traced here: 11.1 us
  Pallas kernels  10.5 us (93%)
  local copies, waits for them, and re-layouts  0.63 us (6%)
    pallas_call x1, Pallas kernels, per_device(): pl.pallas_call(functools.partial(kernel, dims), out_shape=pltpu.VMEM((gro...  10.5 us
    another operation x1, local copies, waits for them, and re-layouts, per_device(): return jnp.swapaxes(result, 0, 1).reshape(waves, slots_here, 2, channels)  0.63 us

profile of v7, /device:TPU:0, one launch (start us, length us, event | category | flops | bytes accessed | tf_op | source)
XLA Modules:
  0.0 11.1 jit_solution(11256852418008540365)
XLA Ops:
  0.0 10.5 %shard_map.73 = bf16[1,64,256]{2,1,0:T(8,128)(2,1)S(1)} custom-call(s32[1,8,15]{2,1,0:T(8,128)} %mask_hbm.1, f32[1,8,15]{2,1,0:T(8,128)} %weight_hbm.1, s32[1,32]{1,0:T(1,128)} %bitcast.1, bf16[1,64,256]{2,1,0:T(8,128)(2,1)} %field_hbm.1, bf16[8,256,256]{2,1,0:T(8,128)(2,1)} %basis_hbm.1, f32[32,256]{1,0:T(8,128)} %gain_hbm.1, bf16[2,256,256]{2,1,0:T(8,128)(2,1)} %spectral_hbm.1), custom_call_target="tpu_custom_call" | custom-call | tf_op jit(solution)/shard_map/pallas_call | solution.py:417
  10.5 0.6 %reshape_transpose_reshape.3 = bf16[8,4,2,256]{3,2,1,0:T(2,128)(2,1)} reshape(bf16[1,64,256]{2,1,0:T(8,128)(2,1)S(1)} %shard_map.73) | data formatting | bytes 65536 | tf_op jit(solution)/shard_map/reshape;transpose;reshape | solution.py:451

commit v8 on v7

--- a/solution.py
+++ b/solution.py
@@ -75,7 +75,8 @@
     follower = (ord_id & 1) == 0
     half = levels // 2
     top = (levels - 1) * n_lat_dev
-    low = level < half
+    direct = levels - 1
+    low = level < direct
     sibling = (lat_id, ord_id ^ 1)
     per_ready = 1 if chips <= 64 else n_lat_dev
 
@@ -113,16 +114,13 @@
 
     @pl.when(chip == 0)
     def _():
-        pl.loop(half * n_lat_dev, chips)(lambda other: greet(device(other, 0)))
+        pl.loop(direct * n_lat_dev, chips)(lambda other: greet(device(other, 0)))
 
     @pl.when(level == levels - 1)
     def _():
-        pl.loop(0, half * n_lat_dev)(lambda other: greet(device(other, 0)))
+        pl.loop(0, direct * n_lat_dev)(lambda other: greet(device(other, 0)))
 
     smem_copy.start()
-    basis_copy.start()
-    gain_copy.start()
-    spectral_copy.start()
 
     filt[pl.ds(0, 1)] = jnp.zeros((1, LANES), F32)
     filt[pl.ds(n_lat + 1, 1)] = jnp.zeros((1, LANES), F32)
@@ -215,12 +213,16 @@
         repeat(2 * n_orders // block_rows, transform)
         send_first()
 
+    basis_copy.start()
+    gain_copy.start()
+    spectral_copy.start()
+
     @pl.when(leader)
     def _():
         pl.semaphore_wait(barrier, 2 * chip + 1)
         signal(known_sem, sibling)
         block = chip // per_ready
-        first = jnp.where(level == levels - 1, half * n_lat_dev, 0)
+        first = jnp.where(level == levels - 1, direct * n_lat_dev, 0)
         pl.loop(first, chip)(lambda other: on_both(other, lambda target: signal(ready.at[block], target)))
 
     @pl.when(follower)

time: 11.3 us -> 11.3 us (level)
  no operation moved by 1% of the time
where the time goes in v8:
time: 11.3 us; the launch traced here: 11.1 us
  Pallas kernels  10.5 us (93%)
  local copies, waits for them, and re-layouts  0.63 us (6%)
    pallas_call x1, Pallas kernels, per_device(): pl.pallas_call(functools.partial(kernel, dims), out_shape=pltpu.VMEM((gro...  10.5 us
    another operation x1, local copies, waits for them, and re-layouts, per_device(): return jnp.swapaxes(result, 0, 1).reshape(waves, slots_here, 2, channels)  0.63 us

profile of v8, /device:TPU:0, one launch (start us, length us, event | category | flops | bytes accessed | tf_op | source)
XLA Modules:
  0.0 11.1 jit_solution(13329220935795359569)
XLA Ops:
  0.0 10.5 %shard_map.73 = bf16[1,64,256]{2,1,0:T(8,128)(2,1)S(1)} custom-call(s32[1,8,15]{2,1,0:T(8,128)} %mask_hbm.1, f32[1,8,15]{2,1,0:T(8,128)} %weight_hbm.1, s32[1,32]{1,0:T(1,128)} %bitcast.1, bf16[1,64,256]{2,1,0:T(8,128)(2,1)} %field_hbm.1, bf16[8,256,256]{2,1,0:T(8,128)(2,1)} %basis_hbm.1, f32[32,256]{1,0:T(8,128)} %gain_hbm.1, bf16[2,256,256]{2,1,0:T(8,128)(2,1)} %spectral_hbm.1), custom_call_target="tpu_custom_call" | custom-call | tf_op jit(solution)/shard_map/pallas_call | solution.py:419
  10.5 0.6 %reshape_transpose_reshape.3 = bf16[8,4,2,256]{3,2,1,0:T(2,128)(2,1)} reshape(bf16[1,64,256]{2,1,0:T(8,128)(2,1)S(1)} %shard_map.73) | data formatting | bytes 65536 | tf_op jit(solution)/shard_map/reshape;transpose;reshape | solution.py:453

commit v9 on v7

--- a/solution.py
+++ b/solution.py
@@ -124,6 +124,13 @@
     gain_copy.start()
     spectral_copy.start()
 
+    early_sem, known_sem, top_sem = ready.at[chips // per_ready], ready.at[chips // per_ready + 1], ready.at[chips // per_ready + 2]
+
+    @pl.when(jnp.logical_and(follower, jnp.logical_not(low)))
+    def _():
+        pl.semaphore_wait(barrier, 3)
+        signal(early_sem, sibling)
+
     filt[pl.ds(0, 1)] = jnp.zeros((1, LANES), F32)
     filt[pl.ds(n_lat + 1, 1)] = jnp.zeros((1, LANES), F32)
 
@@ -156,12 +163,6 @@
         send_filters(target)
         send_rows(target)
 
-    early_sem, known_sem, top_sem = ready.at[chips // per_ready], ready.at[chips // per_ready + 1], ready.at[chips // per_ready + 2]
-
-    @pl.when(jnp.logical_and(follower, jnp.logical_not(low)))
-    def _():
-        pl.semaphore_wait(barrier, 3)
-        signal(early_sem, sibling)
 
     @pl.when(jnp.logical_and(leader, jnp.logical_not(low)))
     def _():

time: 11.3 us -> 11.3 us (level)
  no operation moved by 1% of the time
where the time goes in v9:
time: 11.3 us; the launch traced here: 11.1 us
  Pallas kernels  10.5 us (93%)
  local copies, waits for them, and re-layouts  0.63 us (6%)
    pallas_call x1, Pallas kernels, per_device(): pl.pallas_call(functools.partial(kernel, dims), out_shape=pltpu.VMEM((gro...  10.5 us
    another operation x1, local copies, waits for them, and re-layouts, per_device(): return jnp.swapaxes(result, 0, 1).reshape(waves, slots_here, 2, channels)  0.63 us

profile of v9, /device:TPU:0, one launch (start us, length us, event | category | flops | bytes accessed | tf_op | source)
XLA Modules:
  0.0 11.1 jit_solution(17900239991591438120)
XLA Ops:
  0.0 10.5 %shard_map.73 = bf16[1,64,256]{2,1,0:T(8,128)(2,1)S(1)} custom-call(s32[1,8,15]{2,1,0:T(8,128)} %mask_hbm.1, f32[1,8,15]{2,1,0:T(8,128)} %weight_hbm.1, s32[1,32]{1,0:T(1,128)} %bitcast.1, bf16[1,64,256]{2,1,0:T(8,128)(2,1)} %field_hbm.1, bf16[8,256,256]{2,1,0:T(8,128)(2,1)} %basis_hbm.1, f32[32,256]{1,0:T(8,128)} %gain_hbm.1, bf16[2,256,256]{2,1,0:T(8,128)(2,1)} %spectral_hbm.1), custom_call_target="tpu_custom_call" | custom-call | tf_op jit(solution)/shard_map/pallas_call | solution.py:418
  10.5 0.6 %reshape_transpose_reshape.3 = bf16[8,4,2,256]{3,2,1,0:T(2,128)(2,1)} reshape(bf16[1,64,256]{2,1,0:T(8,128)(2,1)S(1)} %shard_map.73) | data formatting | bytes 65536 | tf_op jit(solution)/shard_map/reshape;transpose;reshape | solution.py:452

commit v10 on v8

--- a/solution.py
+++ b/solution.py
@@ -122,6 +122,13 @@
 
     smem_copy.start()
 
+    early_sem, known_sem, top_sem = ready.at[chips // per_ready], ready.at[chips // per_ready + 1], ready.at[chips // per_ready + 2]
+
+    @pl.when(jnp.logical_and(follower, jnp.logical_not(low)))
+    def _():
+        pl.semaphore_wait(barrier, 3)
+        signal(early_sem, sibling)
+
     filt[pl.ds(0, 1)] = jnp.zeros((1, LANES), F32)
     filt[pl.ds(n_lat + 1, 1)] = jnp.zeros((1, LANES), F32)
 
@@ -154,12 +161,6 @@
         send_filters(target)
         send_rows(target)
 
-    early_sem, known_sem, top_sem = ready.at[chips // per_ready], ready.at[chips // per_ready + 1], ready.at[chips // per_ready + 2]
-
-    @pl.when(jnp.logical_and(follower, jnp.logical_not(low)))
-    def _():
-        pl.semaphore_wait(barrier, 3)
-        signal(early_sem, sibling)
 
     @pl.when(jnp.logical_and(leader, jnp.logical_not(low)))
     def _():

time: 11.3 us -> 11.3 us (level)
  no operation moved by 1% of the time
where the time goes in v10:
time: 11.3 us; the launch traced here: 11.1 us
  Pallas kernels  10.5 us (93%)
  local copies, waits for them, and re-layouts  0.63 us (6%)
    pallas_call x1, Pallas kernels, per_device(): pl.pallas_call(functools.partial(kernel, dims), out_shape=pltpu.VMEM((gro...  10.5 us
    another operation x1, local copies, waits for them, and re-layouts, per_device(): return jnp.swapaxes(result, 0, 1).reshape(waves, slots_here, 2, channels)  0.63 us

profile of v10, /device:TPU:0, one launch (start us, length us, event | category | flops | bytes accessed | tf_op | source)
XLA Modules:
  0.0 11.1 jit_solution(17352056793224534573)
XLA Ops:
  0.0 10.5 %shard_map.73 = bf16[1,64,256]{2,1,0:T(8,128)(2,1)S(1)} custom-call(s32[1,8,15]{2,1,0:T(8,128)} %mask_hbm.1, f32[1,8,15]{2,1,0:T(8,128)} %weight_hbm.1, s32[1,32]{1,0:T(1,128)} %bitcast.1, bf16[1,64,256]{2,1,0:T(8,128)(2,1)} %field_hbm.1, bf16[8,256,256]{2,1,0:T(8,128)(2,1)} %basis_hbm.1, f32[32,256]{1,0:T(8,128)} %gain_hbm.1, bf16[2,256,256]{2,1,0:T(8,128)(2,1)} %spectral_hbm.1), custom_call_target="tpu_custom_call" | custom-call | tf_op jit(solution)/shard_map/pallas_call | solution.py:420
  10.5 0.6 %reshape_transpose_reshape.3 = bf16[8,4,2,256]{3,2,1,0:T(2,128)(2,1)} reshape(bf16[1,64,256]{2,1,0:T(8,128)(2,1)S(1)} %shard_map.73) | data formatting | bytes 65536 | tf_op jit(solution)/shard_map/reshape;transpose;reshape | solution.py:454

commit v11 on v9

--- a/solution.py
+++ b/solution.py
@@ -87,7 +87,13 @@
         body(device(other, 0))
 
     slots_copy = pltpu.make_async_copy(slots_hbm, slots_ref, local_sem.at[0])
-    field_copy = pltpu.make_async_copy(field_hbm, field, local_sem.at[1])
+    pieces = 2
+    piece = n_lon // pieces
+
+    def field_copy(part):
+        place = pl.ds(part * piece, piece)
+        return pltpu.make_async_copy(field_hbm.at[:, place], field.at[:, place], local_sem.at[8 + part])
+
     mask_copy = pltpu.make_async_copy(mask_hbm, mask_ref, local_sem.at[2])
     weight_copy = pltpu.make_async_copy(weight_hbm, weight_ref, local_sem.at[3])
     smem_copy = pltpu.make_async_copy(slots_hbm, slots_smem, local_sem.at[4])
@@ -107,7 +113,8 @@
     mask_copy.start()
     weight_copy.start()
     slots_copy.start()
-    field_copy.start()
+    for part in range(pieces):
+        field_copy(part).start()
     greet(sibling)
     pl.loop(chip + 1, chips)(lambda other: greet(device(other, 1)))
 
@@ -189,7 +196,8 @@
         dft_block(0)
     slabs = block_rows // width
 
-    field_copy.wait()
+    for part in range(pieces):
+        field_copy(part).wait()
 
     def transform(block):
         if not single_dft:
@@ -437,7 +445,7 @@
             pltpu.VMEM((3, 2 * (lat_rows + 2), lat_rows * width), BF16),
             pltpu.VMEM((basis_count * out_rows, lat_rows * width), BF16),
             pltpu.VMEM((8, LANES) if single else (basis_count * out_rows, channels), F32),
-            pltpu.SemaphoreType.DMA((8,)),
+            pltpu.SemaphoreType.DMA((10,)),
             pltpu.SemaphoreType.DMA((1,)),
             pltpu.SemaphoreType.DMA((1,)),
             pltpu.SemaphoreType.DMA((1,)),

time: 11.3 us -> 11.3 us (level)
  no operation moved by 1% of the time
where the time goes in v11:
time: 11.3 us; the launch traced here: 11.2 us
  Pallas kernels  10.5 us (93%)
  local copies, waits for them, and re-layouts  0.63 us (6%)
    pallas_call x1, Pallas kernels, per_device(): pl.pallas_call(functools.partial(kernel, dims), out_shape=pltpu.VMEM((gro...  10.5 us
    another operation x1, local copies, waits for them, and re-layouts, per_device(): return jnp.swapaxes(result, 0, 1).reshape(waves, slots_here, 2, channels)  0.63 us

profile of v11, /device:TPU:0, one launch (start us, length us, event | category | flops | bytes accessed | tf_op | source)
XLA Modules:
  0.0 11.2 jit_solution(12576434660290402788)
XLA Ops:
  0.0 10.5 %shard_map.73 = bf16[1,64,256]{2,1,0:T(8,128)(2,1)S(1)} custom-call(s32[1,8,15]{2,1,0:T(8,128)} %mask_hbm.1, f32[1,8,15]{2,1,0:T(8,128)} %weight_hbm.1, s32[1,32]{1,0:T(1,128)} %bitcast.1, bf16[1,64,256]{2,1,0:T(8,128)(2,1)} %field_hbm.1, bf16[8,256,256]{2,1,0:T(8,128)(2,1)} %basis_hbm.1, f32[32,256]{1,0:T(8,128)} %gain_hbm.1, bf16[2,256,256]{2,1,0:T(8,128)(2,1)} %spectral_hbm.1), custom_call_target="tpu_custom_call" | custom-call | tf_op jit(solution)/shard_map/pallas_call | solution.py:426
  10.5 0.6 %reshape_transpose_reshape.3 = bf16[8,4,2,256]{3,2,1,0:T(2,128)(2,1)} reshape(bf16[1,64,256]{2,1,0:T(8,128)(2,1)S(1)} %shard_map.73) | data formatting | bytes 65536 | tf_op jit(solution)/shard_map/reshape;transpose;reshape | solution.py:460

commit v12 on v11

--- a/solution.py
+++ b/solution.py
@@ -273,7 +273,7 @@
     window_lat = iota((lat_rows + 2, cols), 1) >> log2(width)
     for step in range(3):
         chosen = (window_row == window_lat + 2 - step).astype(F32)
-        select[step] = jnp.concatenate([chosen, chosen], axis=0).astype(BF16)
+        select[step] = chosen.astype(BF16)
 
     single_lat = groups == 1 and parts == 1
     if single_lat:
@@ -338,9 +338,7 @@
 
     def build_left(part, factors):
         window = filt[pl.ds(part * lat_rows, lat_rows + 2)]
-        high = window.astype(BF16)
-        low = (window - high.astype(F32)).astype(BF16)
-        both = jnp.concatenate([high.astype(F32), low.astype(F32)], axis=0).T.astype(BF16)
+        both = window.T.astype(BF16)
         real, imag = [], []
         for step in range(3):
             first = 5 * step * basis_count
@@ -442,7 +440,7 @@
             pltpu.VMEM((n_ord_dev * groups, width, channels), BF16),
             pltpu.VMEM((groups, n_lat, width, channels), BF16),
             pltpu.VMEM((3, out_rows, lat_rows * width), F32),
-            pltpu.VMEM((3, 2 * (lat_rows + 2), lat_rows * width), BF16),
+            pltpu.VMEM((3, lat_rows + 2, lat_rows * width), BF16),
             pltpu.VMEM((basis_count * out_rows, lat_rows * width), BF16),
             pltpu.VMEM((8, LANES) if single else (basis_count * out_rows, channels), F32),
             pltpu.SemaphoreType.DMA((10,)),

time: 11.3 us -> 11.3 us (level)
  no operation moved by 1% of the time
where the time goes in v12:
time: 11.3 us; the launch traced here: 11.2 us
  Pallas kernels  10.5 us (93%)
  local copies, waits for them, and re-layouts  0.63 us (6%)
    pallas_call x1, Pallas kernels, per_device(): pl.pallas_call(functools.partial(kernel, dims), out_shape=pltpu.VMEM((gro...  10.5 us
    another operation x1, local copies, waits for them, and re-layouts, per_device(): return jnp.swapaxes(result, 0, 1).reshape(waves, slots_here, 2, channels)  0.63 us

profile of v12, /device:TPU:0, one launch (start us, length us, event | category | flops | bytes accessed | tf_op | source)
XLA Modules:
  0.0 11.2 jit_solution(3042881106494037938)
XLA Ops:
  0.0 10.5 %shard_map.73 = bf16[1,64,256]{2,1,0:T(8,128)(2,1)S(1)} custom-call(s32[1,8,15]{2,1,0:T(8,128)} %mask_hbm.1, f32[1,8,15]{2,1,0:T(8,128)} %weight_hbm.1, s32[1,32]{1,0:T(1,128)} %bitcast.1, bf16[1,64,256]{2,1,0:T(8,128)(2,1)} %field_hbm.1, bf16[8,256,256]{2,1,0:T(8,128)(2,1)} %basis_hbm.1, f32[32,256]{1,0:T(8,128)} %gain_hbm.1, bf16[2,256,256]{2,1,0:T(8,128)(2,1)} %spectral_hbm.1), custom_call_target="tpu_custom_call" | custom-call | tf_op jit(solution)/shard_map/pallas_call | solution.py:424
  10.5 0.6 %reshape_transpose_reshape.3 = bf16[8,4,2,256]{3,2,1,0:T(2,128)(2,1)} reshape(bf16[1,64,256]{2,1,0:T(8,128)(2,1)S(1)} %shard_map.73) | data formatting | bytes 65536 | tf_op jit(solution)/shard_map/reshape;transpose;reshape | solution.py:458
